TPU v7x, 32 devices: a whole 2x2x4 slice. The times are simulated.
32 devices in a mesh: row: 4 (over z), col: 8 (over y, x, core).
Axes of the slice: x: 2, y: 2, z: 4, core: 2. Of those that a mesh axis runs over, the one named last changes fastest.
Arguments:
- config: float32 [6, 4096], P(None, ('row', 'col')), as said below
- start: float32 [6, 4096], P(None, ('row', 'col')), may hold values from -6 to 6
- tile_list: int32 [4, 8, 8, 5], P('row', 'col'), may hold values from -1 to 7, as said below
- tile_count: int32 [4, 8], P('row', 'col'), may hold values from 1 to 8, as said below
Outputs:
- coefficients: float32 [4], replicated
- mode: float32 [6, 4096], P(None, ('row', 'col'))
Inputs may be any that keep to these rules, and one draw needn't show every extreme that they name: `tile_list`: entry k of device (r, c) is used when k < tile_count[r, c]; its first value is a row tile 0 to 7, its second a column tile 0 to 3, the last three are offsets in -1, 0, 1, not all zero. Unused entries hold values of the same law. `tile_count`: some device uses all 8 entries. `config`: rows 3 to 5 are unit vectors. No two ellipsoids intersect, within a tile or across tiles placed by a list entry's offsets.
All inputs are finite; a program needn't handle non-finite values.
Results may differ from a plain program's by a relative error of at most 0.0003.
Values sent between devices are 32-bit elements; how exact they have to be, the bound alone decides.
No kernel may reach another device: no remote copies, remote signals or barrier semaphores. Data moves between devices by JAX's collectives and lax.ppermute only.
A program may use at most 64 MiB of HBM per device.

v0:
```python
import math

import jax
import jax.numpy as jnp
from jax import lax
from jax.sharding import PartitionSpec as P

chi_shape = 0.8
chi_energy = (math.sqrt(5.0) - 1.0) / (math.sqrt(5.0) + 1.0)
well_depth = 0.005
cutoff_sq = 20.25
norm_eps = 1e-06


def rotate(heading, turn):
    moved = heading + jnp.cross(turn, heading, axis=0)
    return moved / jnp.sqrt(jnp.sum(moved * moved, axis=0, keepdims=True))


def place(frame, dof):
    return (frame[:3] + dof[:3], rotate(frame[3:], dof[3:]))


def pair_energy(separation, left_axis, right_axis):
    distance_sq = jnp.sum(separation * separation, axis=0)
    distance = jnp.sqrt(distance_sq)
    direction = separation / distance
    along_left = jnp.sum(direction * left_axis, axis=0)
    along_right = jnp.sum(direction * right_axis, axis=0)
    cosine = jnp.sum(left_axis * right_axis, axis=0)
    summed_sq = (along_left + along_right) ** 2
    differ_sq = (along_left - along_right) ** 2
    shape_term = 1.0 - 0.5 * chi_shape * (
        summed_sq / (1.0 + chi_shape * cosine) + differ_sq / (1.0 - chi_shape * cosine)
    )
    contact = 1.0 / jnp.sqrt(shape_term)
    strength_one = 1.0 / jnp.sqrt(1.0 - chi_shape * chi_shape * cosine * cosine)
    strength_two = 1.0 - 0.5 * chi_energy * (
        summed_sq / (1.0 + chi_energy * cosine) + differ_sq / (1.0 - chi_energy * cosine)
    )
    reduced = 1.0 / (distance - contact + 1.0)
    sixth = reduced**6
    switch = jnp.maximum(1.0 - distance_sq / cutoff_sq, 0.0) ** 3
    return (
        4.0
        * well_depth
        * strength_one
        * strength_two
        * strength_two
        * (sixth * sixth - sixth)
        * switch
    )


def cross_energy(dof_left, dof_right, left_frame, right_frame, brick_shift):
    left_centre, left_axis = place(left_frame, dof_left)
    right_centre, right_axis = place(right_frame, dof_right)
    separation = right_centre[:, None, :] + brick_shift[:, None, None] - left_centre[:, :, None]
    return jnp.sum(pair_energy(separation, left_axis[:, :, None], right_axis[:, None, :]))


def own_energy(dof, frame):
    centre, heading = place(frame, dof)
    ordinal = lax.iota(jnp.int32, frame.shape[1])
    upper_mask = (ordinal[:, None] < ordinal[None, :]).astype(frame.dtype)
    diagonal = (ordinal[:, None] == ordinal[None, :]).astype(frame.dtype)
    separation = centre[:, None, :] - centre[:, :, None]
    lifted = separation + jnp.stack([0.0 * diagonal, 0.0 * diagonal, 8.0 * diagonal])
    return jnp.sum(upper_mask * pair_energy(lifted, heading[:, :, None], heading[:, None, :]))


def cross_product(left_frame, right_frame, left_tangent, right_tangent, brick_shift):

    def cross_gradient(dof_left, dof_right):
        return jax.grad(cross_energy, argnums=(0, 1))(
            dof_left, dof_right, left_frame, right_frame, brick_shift
        )

    anchor = (jnp.zeros_like(left_tangent), jnp.zeros_like(right_tangent))
    _, tangent = jax.jvp(cross_gradient, anchor, (left_tangent, right_tangent))
    return tangent


def own_product(frame, vector):

    def own_gradient(dof):
        return jax.grad(own_energy)(dof, frame)

    _, tangent = jax.jvp(own_gradient, (jnp.zeros_like(vector),), (vector,))
    return tangent


def local(config, start, tile_list, tile_count):
    member = config.shape[1]
    row_devices = lax.axis_size("row")
    col_devices = lax.axis_size("col")
    total_entries = 6 * member * row_devices * col_devices
    period = jnp.array([5.0, 5.0, 3.5 * (member // 16)], dtype=jnp.float32)
    row_frames = lax.all_gather(config, "col", axis=1, tiled=True)
    col_frames = lax.all_gather(config, "row", axis=1, tiled=True)
    entries = tile_list[0, 0]
    used = tile_count[0, 0]

    def apply_hessian(vector):
        own_term = own_product(config, vector)
        row_vectors = lax.all_gather(vector, "col", axis=1, tiled=True)
        col_vectors = lax.all_gather(vector, "row", axis=1, tiled=True)

        def visit(slot, totals):
            row_total, col_total = totals
            entry = entries[slot]
            left = entry[0] * member
            right = entry[1] * member
            brick_shift = entry[2:5].astype(jnp.float32) * period
            left_out, right_out = cross_product(
                lax.dynamic_slice_in_dim(row_frames, left, member, 1),
                lax.dynamic_slice_in_dim(col_frames, right, member, 1),
                lax.dynamic_slice_in_dim(row_vectors, left, member, 1),
                lax.dynamic_slice_in_dim(col_vectors, right, member, 1),
                brick_shift,
            )
            row_total = lax.dynamic_update_slice_in_dim(
                row_total, lax.dynamic_slice_in_dim(row_total, left, member, 1) + left_out, left, 1
            )
            col_total = lax.dynamic_update_slice_in_dim(
                col_total,
                lax.dynamic_slice_in_dim(col_total, right, member, 1) + right_out,
                right,
                1,
            )
            return (row_total, col_total)

        row_total, col_total = lax.fori_loop(
            0, used, visit, (jnp.zeros_like(row_vectors), jnp.zeros_like(col_vectors))
        )
        row_sum = lax.psum_scatter(row_total, "col", scatter_dimension=1, tiled=True)
        col_sum = lax.psum_scatter(col_total, "row", scatter_dimension=1, tiled=True)
        outcome = own_term + row_sum + col_sum
        return outcome

    def mean_one(values):
        return lax.psum(jnp.sum(values), ("row", "col")) / total_entries

    def next_vector(image, basis):
        alpha = mean_one(basis * image)
        residual = image - alpha * basis
        residual_sq = mean_one(residual * residual)
        beta = jnp.sqrt(residual_sq + norm_eps)
        return (alpha, beta, residual / beta)

    first = start / jnp.sqrt(mean_one(start * start) + norm_eps)
    alpha_one, beta_one, second = next_vector(apply_hessian(first), first)
    alpha_two, beta_two, mode = next_vector(apply_hessian(second) - beta_one * first, second)
    return (jnp.stack([alpha_one, beta_one, alpha_two, beta_two]), mode)


def solution(mesh):
    placed = (
        P(None, ("row", "col")),
        P(None, ("row", "col")),
        P("row", "col", None, None),
        P("row", "col"),
    )
    return jax.shard_map(
        local, mesh=mesh, in_specs=placed, out_specs=(P(), P(None, ("row", "col"))), check_vma=False
    )
```

profile of v0, /device:TPU:0, one launch (start us, length us, event | category | flops | bytes accessed | tf_op | source)
XLA Modules:
  0.0 499.4 jit_solution(6576906539669336353)
XLA Ops:
  7.2 1.3 multiply_reduce_fusion.39
  8.5 42.2 %psum.35 = f32[]{:T(128)} all-reduce(f32[]{:T(128)} %multiply_reduce_fusion.39), channel_id=1, replica_groups=mesh['row'=4,'col'=8] {'row','col'}, use_global_device_ids=true, to_apply=%region_1.0 | all-reduce | flops 1 | bytes 8 | tf_op jit(solution)/shard_map/psum | solution.py:142
  51.4 10.0 %all_gather.19 = f32[6,1024]{1,0:T(8,128)S(1)} all-gather(f32[6,128]{1,0:T(8,128)S(1)} %broadcast_divide_fusion.23), channel_id=1, replica_groups=mesh['row'=4,'col'=8] {'col'}, dimensions={1}, use_global_device_ids=true | all-gather | bytes 27648 | tf_op jit(solution)/shard_map/all_gather | solution.py:106
  61.5 13.2 %all_gather.21 = f32[6,512]{1,0:T(8,128)S(1)} all-gather(f32[6,128]{1,0:T(8,128)S(1)} %broadcast_divide_fusion.23), channel_id=1, replica_groups=mesh['row'=4,'col'=8] {'row'}, dimensions={1}, use_global_device_ids=true | all-gather | bytes 15360 | tf_op jit(solution)/shard_map/all_gather | solution.py:107
  74.7 8.1 %all_gather.18 = f32[6,1024]{1,0:T(8,128)S(1)} all-gather(f32[6,128]{1,0:T(8,128)S(1)} %copy-done.5), channel_id=1, replica_groups=mesh['row'=4,'col'=8] {'col'}, dimensions={1}, use_global_device_ids=true | all-gather | bytes 27648 | tf_op jit(solution)/shard_map/all_gather | solution.py:99
  82.8 13.2 %all_gather.20 = f32[6,512]{1,0:T(8,128)S(1)} all-gather(f32[6,128]{1,0:T(8,128)S(1)} %copy-done.5), channel_id=1, replica_groups=mesh['row'=4,'col'=8] {'row'}, dimensions={1}, use_global_device_ids=true | all-gather | bytes 15360 | tf_op jit(solution)/shard_map/all_gather | solution.py:100
  96.1 0.7 copy-done.7
  96.8 7.0 %while.26 = (s32[]{:T(128)}, f32[6,1024]{1,0:T(8,128)S(1)}, f32[6,512]{1,0:T(8,128)S(1)}, s32[]{:T(128)}, s32[8,5]{1,0:T(8,128)S(1)}, /*index=5*/f32[6,1024]{1,0...) while((s32[]{:T(128)}, f32[6,1024]{1,0:T(8,128)S(1)}, ...), condition=%wide.region_55.60_spmd.clone, body=%wide.region_26.59_spmd.sunk.clone.sunk | while | flops 15415315 | bytes 7267735 | solution.py:133
  97.5 0.6 fusion.369
  100.3 0.7 fusion.374
  101.6 0.6 add_reduce_fusion.39
  104.5 0.7 reduce-scatter.5.cloned.1.call-update
  105.9 0.6 negate_add_fusion.8
  108.6 55.7 %reduce-scatter.7.cloned.1.call-done = f32[6,128]{1,0:T(8,128)} async-done(((f32[6,512]{1,0:T(8,128)}), f32[6,128]{1,0:T(8,128)}) %reduce-scatter.7.cloned.1.call-update) | async-done | bytes 3088 | tf_op jit(solution)/shard_map/reduce_scatter | solution.py:137
  164.2 32.8 %reduce-scatter.5.cloned.1.call-done = f32[6,128]{1,0:T(8,128)} async-done(((f32[6,1024]{1,0:T(8,128)}), f32[6,128]{1,0:T(8,128)}) %reduce-scatter.5.cloned.1.call-update) | async-done | bytes 3088 | tf_op jit(solution)/shard_map/reduce_scatter | solution.py:136
  197.0 1.3 multiply_reduce_fusion.38
  198.3 39.5 %psum.36 = f32[]{:T(128)} all-reduce(f32[]{:T(128)} %get-tuple-element.458), channel_id=1, replica_groups=mesh['row'=4,'col'=8] {'row','col'}, use_global_device_ids=true, to_apply=%region_59.64 | all-reduce | flops 1 | bytes 8 | tf_op jit(solution)/shard_map/psum | solution.py:142
  238.5 0.6 multiply_reduce_fusion.37
  239.1 41.4 %psum.37 = f32[]{:T(128)} all-reduce(f32[]{:T(128)} %multiply_reduce_fusion.37), channel_id=1, replica_groups=mesh['row'=4,'col'=8] {'row','col'}, use_global_device_ids=true, to_apply=%region_61.66 | all-reduce | flops 1 | bytes 8 | tf_op jit(solution)/shard_map/psum | solution.py:142
  281.2 10.0 %all_gather.22 = f32[6,1024]{1,0:T(8,128)S(1)} all-gather(f32[6,128]{1,0:T(8,128)S(1)} %broadcast_divide_fusion.22), channel_id=1, replica_groups=mesh['row'=4,'col'=8] {'col'}, dimensions={1}, use_global_device_ids=true | all-gather | bytes 27648 | tf_op jit(solution)/shard_map/all_gather | solution.py:106
  291.3 13.3 %all_gather.23 = f32[6,512]{1,0:T(8,128)S(1)} all-gather(f32[6,128]{1,0:T(8,128)S(1)} %broadcast_divide_fusion.22), channel_id=1, replica_groups=mesh['row'=4,'col'=8] {'row'}, dimensions={1}, use_global_device_ids=true | all-gather | bytes 15360 | tf_op jit(solution)/shard_map/all_gather | solution.py:107
  307.4 7.0 %while.27 = (s32[]{:T(128)}, f32[6,1024]{1,0:T(8,128)S(1)}, f32[6,512]{1,0:T(8,128)S(1)}, s32[]{:T(128)}, s32[8,5]{1,0:T(8,128)S(1)}, /*index=5*/f32[6,1024]{1,0...) while((s32[]{:T(128)}, f32[6,1024]{1,0:T(8,128)S(1)}, ...), condition=%wide.region_114.0_spmd.clone, body=%wide.region_85.118_spmd.sunk.clone.sunk | while | flops 15415315 | bytes 7267735 | solution.py:133
  308.1 0.6 fusion.380
  311.0 0.7 fusion.385
  312.2 0.6 add_reduce_fusion.41
  315.7 59.3 %reduce-scatter.11.cloned.1.call-done = f32[6,128]{1,0:T(8,128)} async-done(((f32[6,512]{1,0:T(8,128)}), f32[6,128]{1,0:T(8,128)}) %reduce-scatter.11.cloned.1.call-update) | async-done | bytes 3088 | tf_op jit(solution)/shard_map/reduce_scatter | solution.py:137
  375.0 32.6 %reduce-scatter.9.cloned.1.call-done = f32[6,128]{1,0:T(8,128)} async-done(((f32[6,1024]{1,0:T(8,128)}), f32[6,128]{1,0:T(8,128)}) %reduce-scatter.9.cloned.1.call-update) | async-done | bytes 3088 | tf_op jit(solution)/shard_map/reduce_scatter | solution.py:136
  407.6 1.3 multiply_reduce_fusion.36
  408.8 39.5 %psum.38 = f32[]{:T(128)} all-reduce(f32[]{:T(128)} %get-tuple-element.446), channel_id=1, replica_groups=mesh['row'=4,'col'=8] {'row','col'}, use_global_device_ids=true, to_apply=%region_118.0 | all-reduce | flops 1 | bytes 8 | tf_op jit(solution)/shard_map/psum | solution.py:142
  449.0 0.6 multiply_reduce_fusion.35
  449.6 41.4 %psum.39 = f32[]{:T(128)} all-reduce(f32[]{:T(128)} %multiply_reduce_fusion.35), channel_id=1, replica_groups=mesh['row'=4,'col'=8] {'row','col'}, use_global_device_ids=true, to_apply=%region_120.0 | all-reduce | flops 1 | bytes 8 | tf_op jit(solution)/shard_map/psum | solution.py:142
  491.7 0.6 broadcast_divide_fusion.21
  (150 shorter events, 12.5 us)
Async XLA Ops:
  7.2 157.1 %reduce-scatter.7.cloned.1.call-start = ((), (), s32[]{:S(2)}) async-start(), calls=%async_computation.5 | async-start | bytes 20480 | tf_op jit(solution)/shard_map/reduce_scatter | solution.py:137
  8.5 42.9 %copy-start.4 = (f32[6,128]{1,0:T(8,128)S(1)}, f32[6,128]{1,0:T(8,128)}, u32[]{:S(2)}) copy-start(f32[6,128]{1,0:T(8,128)} %param.25) | copy-start | bytes 9220
  61.5 13.3 %copy-start.5 = (f32[6,128]{1,0:T(8,128)S(1)}, f32[6,128]{1,0:T(8,128)}, u32[]{:S(2)}) copy-start(f32[6,128]{1,0:T(8,128)} %param.24) | copy-start | bytes 9220
  82.8 13.3 %copy-start.6 = (s32[1,1,8,5]{2,1,3,0:T(1,128)S(1)}, s32[1,1,8,5]{2,1,3,0:T(1,128)}, u32[]{:S(2)}) copy-start(s32[1,1,8,5]{2,1,3,0:T(1,128)} %param.26) | copy-start | bytes 484
  96.1 0.7 copy-start.7
  103.8 0.6 copy-start.3
  103.8 0.7 copy-start.1
  104.4 92.6 %reduce-scatter.5.cloned.1.call-start = ((), (), s32[]{:S(2)}) async-start(), calls=%async_computation.4 | async-start | bytes 36864 | tf_op jit(solution)/shard_map/reduce_scatter | solution.py:136
  105.2 269.8 %reduce-scatter.11.cloned.1.call-start = ((), (), s32[]{:S(2)}) async-start(), calls=%async_computation.7 | async-start | bytes 20480 | tf_op jit(solution)/shard_map/reduce_scatter | solution.py:137
  314.5 0.6 copy-start.2
  314.5 0.7 copy-start
  315.1 92.4 %reduce-scatter.9.cloned.1.call-start = ((), (), s32[]{:S(2)}) async-start(), calls=%async_computation.6 | async-start | bytes 36864 | tf_op jit(solution)/shard_map/reduce_scatter | solution.py:136
Sparse Core Ops, SparseCore 0:
  104.6 59.6 reduce-scatter.6
  167.5 29.4 reduce-scatter.4
  315.2 59.7 reduce-scatter.10
  378.1 29.3 reduce-scatter.8
where the time goes:
time: 502 us; the launch traced here: 499 us
  blocking collectives  272 us (54%)
  waiting for transfers between devices  181 us (36%)
  other arithmetic  19.4 us (4%)
  between operations  17.4 us (3%)
  loops' own time  5.74 us (1%)
    psum x5, blocking collectives, mean_one(): return lax.psum(jnp.sum(values), ('row', 'col')) / total_entries  204 us
    reduce_scatter x2, waiting for transfers between devices, apply_hessian(): lax.psum_scatter(col_total, 'row', scatter_dimension=1, tiled=True)  115 us
    reduce_scatter x2, waiting for transfers between devices, apply_hessian(): lax.psum_scatter(row_total, 'col', scatter_dimension=1, tiled=True)  65.3 us
    all_gather x2, blocking collectives, apply_hessian(): col_vectors = lax.all_gather(vector, 'row', axis=1, tiled=True)  26.5 us
    all_gather x2, blocking collectives, apply_hessian(): row_vectors = lax.all_gather(vector, 'col', axis=1, tiled=True)  20.1 us
    all_gather x1, blocking collectives, local(): col_frames = lax.all_gather(config, 'row', axis=1, tiled=True)  13.2 us
  transfers between devices with their start and end apart: 4, of which 4 were waited for; matrix products, arithmetic and copies ran while one was open for 1% of the time, Pallas kernels for 0%

commit v1 on v0

--- a/solution.py
+++ b/solution.py
@@ -91,67 +91,70 @@
 
 
 def local(config, start, tile_list, tile_count):
-    member = config.shape[1]
+    dof, member = config.shape
     row_devices = lax.axis_size("row")
     col_devices = lax.axis_size("col")
-    total_entries = 6 * member * row_devices * col_devices
+    row_id = lax.axis_index("row")
+    col_id = lax.axis_index("col")
+    total_entries = dof * member * row_devices * col_devices
     period = jnp.array([5.0, 5.0, 3.5 * (member // 16)], dtype=jnp.float32)
-    row_frames = lax.all_gather(config, "col", axis=1, tiled=True)
-    col_frames = lax.all_gather(config, "row", axis=1, tiled=True)
     entries = tile_list[0, 0]
     used = tile_count[0, 0]
 
-    def apply_hessian(vector):
+    def everywhere(values):
+        gathered = lax.all_gather(values, ("row", "col"), axis=0, tiled=False)
+        return gathered.reshape((row_devices, col_devices) + values.shape)
+
+    def mean_of(values):
+        return jnp.sum(values) / total_entries
+
+    together = everywhere(jnp.concatenate([config, start], axis=0))
+    all_start = together[:, :, dof:]
+    row_frames = lax.dynamic_index_in_dim(together, row_id, 0, keepdims=False)[:, :dof]
+    col_frames = lax.dynamic_index_in_dim(together, col_id, 1, keepdims=False)[:, :dof]
+
+    def apply_hessian(vectors):
+        row_vectors = lax.dynamic_index_in_dim(vectors, row_id, 0, keepdims=False)
+        col_vectors = lax.dynamic_index_in_dim(vectors, col_id, 1, keepdims=False)
+        vector = lax.dynamic_index_in_dim(row_vectors, col_id, 0, keepdims=False)
         own_term = own_product(config, vector)
-        row_vectors = lax.all_gather(vector, "col", axis=1, tiled=True)
-        col_vectors = lax.all_gather(vector, "row", axis=1, tiled=True)
 
         def visit(slot, totals):
             row_total, col_total = totals
             entry = entries[slot]
-            left = entry[0] * member
-            right = entry[1] * member
+            left = entry[0]
+            right = entry[1]
             brick_shift = entry[2:5].astype(jnp.float32) * period
             left_out, right_out = cross_product(
-                lax.dynamic_slice_in_dim(row_frames, left, member, 1),
-                lax.dynamic_slice_in_dim(col_frames, right, member, 1),
-                lax.dynamic_slice_in_dim(row_vectors, left, member, 1),
-                lax.dynamic_slice_in_dim(col_vectors, right, member, 1),
+                row_frames[left],
+                col_frames[right],
+                row_vectors[left],
+                col_vectors[right],
                 brick_shift,
             )
-            row_total = lax.dynamic_update_slice_in_dim(
-                row_total, lax.dynamic_slice_in_dim(row_total, left, member, 1) + left_out, left, 1
-            )
-            col_total = lax.dynamic_update_slice_in_dim(
-                col_total,
-                lax.dynamic_slice_in_dim(col_total, right, member, 1) + right_out,
-                right,
-                1,
-            )
-            return (row_total, col_total)
+            return (row_total.at[left].add(left_out), col_total.at[right].add(right_out))
 
         row_total, col_total = lax.fori_loop(
             0, used, visit, (jnp.zeros_like(row_vectors), jnp.zeros_like(col_vectors))
         )
-        row_sum = lax.psum_scatter(row_total, "col", scatter_dimension=1, tiled=True)
-        col_sum = lax.psum_scatter(col_total, "row", scatter_dimension=1, tiled=True)
-        outcome = own_term + row_sum + col_sum
-        return outcome
-
-    def mean_one(values):
-        return lax.psum(jnp.sum(values), ("row", "col")) / total_entries
+        row_sum = lax.psum_scatter(row_total, "col", scatter_dimension=0, tiled=False)
+        col_sum = lax.psum_scatter(col_total, "row", scatter_dimension=0, tiled=False)
+        return own_term + row_sum + col_sum
 
     def next_vector(image, basis):
-        alpha = mean_one(basis * image)
+        alpha = mean_of(basis * image)
         residual = image - alpha * basis
-        residual_sq = mean_one(residual * residual)
-        beta = jnp.sqrt(residual_sq + norm_eps)
+        beta = jnp.sqrt(mean_of(residual * residual) + norm_eps)
         return (alpha, beta, residual / beta)
 
-    first = start / jnp.sqrt(mean_one(start * start) + norm_eps)
-    alpha_one, beta_one, second = next_vector(apply_hessian(first), first)
-    alpha_two, beta_two, mode = next_vector(apply_hessian(second) - beta_one * first, second)
-    return (jnp.stack([alpha_one, beta_one, alpha_two, beta_two]), mode)
+    def mine(values):
+        return values[row_id, col_id]
+
+    first = all_start / jnp.sqrt(mean_of(all_start * all_start) + norm_eps)
+    alpha_one, beta_one, second = next_vector(everywhere(apply_hessian(first)), first)
+    image = apply_hessian(second) - beta_one * mine(first)
+    alpha_two, beta_two, mode = next_vector(everywhere(image), second)
+    return (jnp.stack([alpha_one, beta_one, alpha_two, beta_two]), mine(mode))
 
 
 def solution(mesh):

time: 502 us -> 399 us (0.79)
  waiting for transfers between devices: 181 us -> 0 us
  other arithmetic: 19.4 us -> 100 us
  loops' own time: 5.74 us -> 65.7 us
  blocking collectives: 272 us -> 216 us
  between operations: 17.4 us -> 4.33 us
  local copies, waits for them, and re-layouts: 3.26 us -> 14.9 us
    psum x5 -> x0, blocking collectives: 204 us -> none  [mean_one(): return lax.psum(jnp.sum(values), ('row', 'col')) / total_entries]
    reduce_scatter x4 -> x0, waiting for transfers between devices: 180 us -> none  [the longest x2 115 us: apply_hessian(): lax.psum_scatter(col_total, 'row', scatter_dimension=1, tiled=True)]
    unnamed x0 -> x4, blocking collectives: none -> 98.9 us
    another operation x2, loops' own time: 5.74 us -> 65.7 us  [apply_hessian(): lax.fori_loop(0, used, visit, (jnp.zeros_like(row_vectors), jnp.zeros_lik...]
    all_gather x6 -> x3, blocking collectives: 67.9 us -> 117 us  [everywhere(): gathered = lax.all_gather(values, ('row', 'col'), axis=0, tiled=False)]
    another operation x1 -> x29, other arithmetic: 0.59 us -> 21.3 us  [local(): return (jnp.stack([alpha_one, beta_one, alpha_two, beta_two]), mode)]
    scatter-add x0 -> x14, other arithmetic: none -> 17.1 us  [visit(): row_total.at[left].add(left_out)]
    reduce_sum x8 -> x32, other arithmetic: 3.24 us -> 13.8 us  [pair_energy(): along_right = jnp.sum(direction * right_axis, axis=0)]
  transfers between devices with their start and end apart: 4 -> 0, of which waited for: 4 -> 0; matrix products, arithmetic and copies ran while one was open for 1% -> 0% of each run, Pallas kernels for 0% -> 0%
where the time goes in v1:
time: 399 us; the launch traced here: 401 us
  blocking collectives  216 us (54%)
  other arithmetic  100 us (25%)
  loops' own time  65.7 us (16%)
  local copies, waits for them, and re-layouts  14.9 us (4%)
  between operations  4.33 us (1%)
    all_gather x3, blocking collectives, everywhere(): gathered = lax.all_gather(values, ('row', 'col'), axis=0, tiled=False)  117 us
    unnamed x4, blocking collectives  98.9 us
    another operation x2, loops' own time, apply_hessian(): lax.fori_loop(0, used, visit, (jnp.zeros_like(row_vectors), jnp.zeros_lik...  65.7 us
    another operation x28, other arithmetic  20.7 us
    scatter-add x14, other arithmetic, visit(): row_total.at[left].add(left_out)  17.1 us
    reduce_sum x32, other arithmetic, pair_energy(): along_right = jnp.sum(direction * right_axis, axis=0)  13.8 us
    add_any x14, other arithmetic, pair_energy(): chi_shape * cosine  9.53 us
    add_any x47, other arithmetic, pair_energy(): summed_sq = (along_left + along_right) ** 2  9.31 us

profile of v1, /device:TPU:0, one launch (start us, length us, event | category | flops | bytes accessed | tf_op | source)
XLA Modules:
  0.0 401.3 jit_solution(2448667168385540127)
XLA Ops:
  1.3 43.9 %all-gather.3 = f32[32,12,128]{2,1,0:T(8,128)S(1)} all-gather(f32[1,12,128]{2,1,0:T(8,128)S(1)} %maximum_bitcast_fusion), channel_id=2, replica_groups=mesh['row'=4,'col'=8] {'row','col'}, dimensions={0}, use_global_device_ids=true | all-gather | bytes 202752 | tf_op jit(solution)/shard_map/all_gather | solution.py:105
  52.8 79.4 %while.30 = (s32[]{:T(128)}, f32[8,6,128]{2,1,0:T(8,128)S(1)}, f32[4,6,128]{2,1,0:T(8,128)S(1)}, s32[]{:T(128)}, s32[8,5]{1,0:T(8,128)S(1)}, /*index=5*/f32[8,6,...) while((s32[]{:T(128)}, f32[8,6,128]{2,1,0:T(8,128)S(1)}, ...), condition=%wide.region_56.61_spmd.clone, body=%wide.region_25.60_spmd.sunk.clone.sunk | while | flops 15416883 | bytes 7267763 | solution.py:137
  62.9 1.2 fusion.382
  74.1 1.2 fusion.382
  85.3 1.2 fusion.382
  96.6 1.2 fusion.382
  107.8 1.2 fusion.382
  119.1 1.2 fusion.382
  130.3 1.2 fusion.382
  132.2 33.8 %all-reduce.21 = f32[8,6,128]{2,1,0:T(8,128)S(1)} all-reduce(f32[8,6,128]{2,1,0:T(8,128)S(1)} %get-tuple-element.198), channel_id=5, replica_groups=mesh['row'=4,'col'=8] {'col'}, use_global_device_ids=true, to_apply=%region_57.62.clone | all-reduce | flops 6144 | bytes 49152
  166.0 15.5 %all-reduce.22 = f32[4,6,128]{2,1,0:T(8,128)S(1)} all-reduce(f32[4,6,128]{2,1,0:T(8,128)S(1)} %get-tuple-element.199), channel_id=6, replica_groups=mesh['row'=4,'col'=8] {'row'}, use_global_device_ids=true, to_apply=%region_58.63.clone | all-reduce | flops 3072 | bytes 24576
  183.9 1.3 fusion.305
  185.3 36.7 %all-gather.4 = f32[32,6,128]{2,1,0:T(8,128)S(1)} all-gather(f32[1,6,128]{2,1,0:T(8,128)S(1)} %fusion.305), channel_id=3, replica_groups=mesh['row'=4,'col'=8] {'row','col'}, dimensions={0}, use_global_device_ids=true | all-gather | bytes 101376 | tf_op jit(solution)/shard_map/all_gather | solution.py:105
  227.7 82.1 %while.31 = (s32[]{:T(128)}, f32[8,6,128]{2,1,0:T(8,128)S(1)}, f32[4,6,128]{2,1,0:T(8,128)S(1)}, s32[]{:T(128)}, s32[8,5]{1,0:T(8,128)S(1)}, /*index=5*/f32[8,6,...) while((s32[]{:T(128)}, f32[8,6,128]{2,1,0:T(8,128)S(1)}, ...), condition=%wide.region_115.120_spmd.clone, body=%wide.region_84.119_spmd.sunk.clone.sunk | while | flops 15416883 | bytes 7267763 | solution.py:137
  237.4 0.8 and_reduce_fusion.10
  238.2 1.2 fusion.393
  249.0 0.8 and_reduce_fusion.10
  249.8 1.2 fusion.393
  260.6 0.8 and_reduce_fusion.10
  261.4 1.2 fusion.393
  272.3 0.8 and_reduce_fusion.10
  273.0 1.2 fusion.393
  283.9 0.8 and_reduce_fusion.10
  284.6 1.2 fusion.393
  295.5 0.8 and_reduce_fusion.10
  296.2 1.2 fusion.393
  307.1 0.8 and_reduce_fusion.10
  307.9 1.2 fusion.393
  309.8 34.1 %all-reduce.23 = f32[8,6,128]{2,1,0:T(8,128)S(1)} all-reduce(f32[8,6,128]{2,1,0:T(8,128)S(1)} %get-tuple-element.205), channel_id=7, replica_groups=mesh['row'=4,'col'=8] {'col'}, use_global_device_ids=true, to_apply=%region_116.121.clone | all-reduce | flops 6144 | bytes 49152
  343.9 15.5 %all-reduce.24 = f32[4,6,128]{2,1,0:T(8,128)S(1)} all-reduce(f32[4,6,128]{2,1,0:T(8,128)S(1)} %get-tuple-element.206), channel_id=8, replica_groups=mesh['row'=4,'col'=8] {'row'}, use_global_device_ids=true, to_apply=%region_117.122.clone | all-reduce | flops 3072 | bytes 24576
  359.4 1.3 fusion.304
  360.7 36.7 %all-gather.5 = f32[32,6,128]{2,1,0:T(8,128)S(1)} all-gather(f32[1,6,128]{2,1,0:T(8,128)S(1)} %fusion.304), channel_id=4, replica_groups=mesh['row'=4,'col'=8] {'row','col'}, dimensions={0}, use_global_device_ids=true | all-gather | bytes 101376 | tf_op jit(solution)/shard_map/all_gather | solution.py:105
  (674 shorter events, 89.9 us)
Async XLA Ops:
  46.6 0.7 copy-start.4
  50.7 0.6 copy-start.1
  51.3 0.8 copy-start.3
  51.3 0.8 copy-start.6
  51.3 0.6 copy-start
  51.3 0.7 copy-start.5
  52.0 0.8 slice-start.1
  52.1 0.7 slice-start
  52.1 0.7 copy-start.2
  181.5 0.7 copy-start.8
  182.7 0.7 copy-start.7

commit v2 on v1

--- a/solution.py
+++ b/solution.py
@@ -101,9 +101,15 @@
     entries = tile_list[0, 0]
     used = tile_count[0, 0]
 
+    def along(values, name, size):
+        arrived = [values]
+        for step in range(1, size):
+            pairs = [(at, (at - step) % size) for at in range(size)]
+            arrived.append(lax.ppermute(values, name, pairs))
+        return jnp.roll(jnp.stack(arrived), lax.axis_index(name), axis=0)
+
     def everywhere(values):
-        gathered = lax.all_gather(values, ("row", "col"), axis=0, tiled=False)
-        return gathered.reshape((row_devices, col_devices) + values.shape)
+        return along(along(values, "col", col_devices), "row", row_devices)
 
     def mean_of(values):
         return jnp.sum(values) / total_entries

time: 399 us -> 334 us (0.84)
  blocking collectives: 216 us -> 164 us
  starting transfers between devices: 0 us -> 38.5 us
  other arithmetic: 100 us -> 63.3 us
  loops' own time: 65.7 us -> 38.3 us
  waiting for transfers between devices: 0 us -> 21.5 us
  local copies, waits for them, and re-layouts: 14.9 us -> 9.51 us
    all_gather x3 -> x0, blocking collectives: 117 us -> none  [everywhere(): gathered = lax.all_gather(values, ('row', 'col'), axis=0, tiled=False)]
    unnamed x4, blocking collectives: 98.9 us -> 164 us
    ppermute x0 -> x30, starting transfers between devices: none -> 38.5 us  [along(): arrived.append(lax.ppermute(values, name, pairs))]
    another operation x2, loops' own time: 65.7 us -> 38.3 us  [apply_hessian(): lax.fori_loop(0, used, visit, (jnp.zeros_like(row_vectors), jnp.zeros_lik...]
    ppermute x0 -> x30, waiting for transfers between devices: none -> 21.5 us  [along(): arrived.append(lax.ppermute(values, name, pairs))]
    another operation x28 -> x18, other arithmetic: 20.7 us -> 11.9 us
    scatter-add x14 -> x8, other arithmetic: 17.1 us -> 9.78 us  [visit(): row_total.at[left].add(left_out)]
    reduce_sum x32 -> x20, other arithmetic: 13.8 us -> 8.48 us  [pair_energy(): along_right = jnp.sum(direction * right_axis, axis=0)]
  transfers between devices with their start and end apart: 0 -> 30, of which waited for: 0 -> 13; matrix products, arithmetic and copies ran while one was open for 0% -> 0% of each run, Pallas kernels for 0% -> 0%
where the time goes in v2:
time: 334 us; the launch traced here: 340 us
  blocking collectives  164 us (49%)
  other arithmetic  63.3 us (19%)
  starting transfers between devices  38.5 us (12%)
  loops' own time  38.3 us (11%)
  waiting for transfers between devices  21.5 us (6%)
  local copies, waits for them, and re-layouts  9.51 us (3%)
  between operations  4.73 us (1%)
    unnamed x4, blocking collectives  164 us
    ppermute x30, starting transfers between devices, along(): arrived.append(lax.ppermute(values, name, pairs))  38.5 us
    another operation x2, loops' own time, apply_hessian(): lax.fori_loop(0, used, visit, (jnp.zeros_like(row_vectors), jnp.zeros_lik...  38.3 us
    ppermute x30, waiting for transfers between devices, along(): arrived.append(lax.ppermute(values, name, pairs))  21.5 us
    another operation x16, other arithmetic  11.8 us
    scatter-add x8, other arithmetic, visit(): row_total.at[left].add(left_out)  9.78 us
    reduce_sum x20, other arithmetic, pair_energy(): along_right = jnp.sum(direction * right_axis, axis=0)  8.48 us
  transfers between devices with their start and end apart: 30, of which 13 were waited for; matrix products, arithmetic and copies ran while one was open for 0% of the time, Pallas kernels for 0%

profile of v2, /device:TPU:0, one launch (start us, length us, event | category | flops | bytes accessed | tf_op | source)
XLA Modules:
  0.0 339.5 jit_solution(13241290816612831621)
XLA Ops:
  1.4 3.4 collective-permute-start
  5.7 1.5 collective-permute-start.3
  7.4 2.4 collective-permute-start.5
  10.3 2.1 collective-permute-done.5
  12.4 1.4 collective-permute-done.6
  13.9 3.7 %collective-permute-start.7 = (f32[8,12,128]{2,1,0:T(8,128)S(1)}, f32[8,12,128]{2,1,0:T(8,128)S(1)}, u32[]{:S(2)}, u32[]{:S(2)}) collective-permute-start(f32[8,12,128]{2,1,0:T(8,128)S(1)} %get-tuple-element.542), channel_id=1, source_target_pairs={{0,24},{8,0},{16,8},{24,16},{1,25},{9,1},{17,9},{25,17},{2,26},{10... | collective-permute-start | bytes 147464 | tf_op jit(solution)/shard_map/ppermute | solution.py:108
  21.3 4.1 %collective-permute-done.8 = f32[8,12,128]{2,1,0:T(8,128)S(1)} collective-permute-done((f32[8,12,128]{2,1,0:T(8,128)S(1)}, f32[8,12,128]{2,1,0:T(8,128)S(1)}, u32[]{:S(2)}, u32[]{:S(2)}) %collective-permute-start.8) | collective-permute-done | bytes 49184 | tf_op jit(solution)/shard_map/ppermute | solution.py:108
  29.3 45.5 %while.30 = (s32[]{:T(128)}, f32[8,6,128]{2,1,0:T(8,128)S(1)}, f32[4,6,128]{2,1,0:T(8,128)S(1)}, s32[]{:T(128)}, s32[8,5]{1,0:T(8,128)S(1)}, /*index=5*/f32[8,6,...) while((s32[]{:T(128)}, f32[8,6,128]{2,1,0:T(8,128)S(1)}, ...), condition=%wide.region_56.61_spmd.clone, body=%wide.region_25.60_spmd.sunk.clone.sunk | while | flops 15416883 | bytes 7267771 | solution.py:143
  74.9 15.5 %all-reduce.22 = f32[4,6,128]{2,1,0:T(8,128)S(1)} all-reduce(f32[4,6,128]{2,1,0:T(8,128)S(1)} %get-tuple-element.201), channel_id=3, replica_groups=mesh['row'=4,'col'=8] {'row'}, use_global_device_ids=true, to_apply=%region_58.63.clone | all-reduce | flops 3072 | bytes 24576
  90.4 65.0 %all-reduce.21 = f32[8,6,128]{2,1,0:T(8,128)S(1)} all-reduce(f32[8,6,128]{2,1,0:T(8,128)S(1)} %get-tuple-element.200), channel_id=2, replica_groups=mesh['row'=4,'col'=8] {'col'}, use_global_device_ids=true, to_apply=%region_57.62.clone | all-reduce | flops 6144 | bytes 49152
  158.7 1.3 constant_dynamic-update-slice_fusion.31
  161.0 1.7 collective-permute-start.11
  162.7 1.7 collective-permute-start.12
  164.5 1.4 collective-permute-start.14
  166.0 2.8 collective-permute-start.15
  168.9 1.6 collective-permute-done.15
  170.5 2.3 collective-permute-done.16
  173.1 3.5 %collective-permute-start.17 = (f32[8,6,128]{2,1,0:T(8,128)S(1)}, f32[8,6,128]{2,1,0:T(8,128)S(1)}, u32[]{:S(2)}, u32[]{:S(2)}) collective-permute-start(f32[8,6,128]{2,1,0:T(8,128)S(1)} %fusion.314), channel_id=1, source_target_pairs={{0,24},{8,0},{16,8},{24,16},{1,25},{9,1},{17,9},{25,17},{2,26},{10... | collective-permute-start | bytes 73736 | tf_op jit(solution)/shard_map/ppermute | solution.py:108
  176.7 1.9 collective-permute-done.19
  182.0 47.1 %while.31 = (s32[]{:T(128)}, f32[8,6,128]{2,1,0:T(8,128)S(1)}, f32[4,6,128]{2,1,0:T(8,128)S(1)}, s32[]{:T(128)}, s32[8,5]{1,0:T(8,128)S(1)}, /*index=5*/f32[8,6,...) while((s32[]{:T(128)}, f32[8,6,128]{2,1,0:T(8,128)S(1)}, ...), condition=%wide.region_115.122_spmd.clone, body=%wide.region_84.121_spmd.sunk.clone.sunk | while | flops 15416883 | bytes 7267771 | solution.py:143
  192.5 1.2 fusion.416
  229.1 15.5 %all-reduce.24 = f32[4,6,128]{2,1,0:T(8,128)S(1)} all-reduce(f32[4,6,128]{2,1,0:T(8,128)S(1)} %get-tuple-element.208), channel_id=5, replica_groups=mesh['row'=4,'col'=8] {'row'}, use_global_device_ids=true, to_apply=%region_117.124.clone | all-reduce | flops 3072 | bytes 24576
  244.6 67.6 %all-reduce.23 = f32[8,6,128]{2,1,0:T(8,128)S(1)} all-reduce(f32[8,6,128]{2,1,0:T(8,128)S(1)} %get-tuple-element.207), channel_id=4, replica_groups=mesh['row'=4,'col'=8] {'col'}, use_global_device_ids=true, to_apply=%region_116.123.clone | all-reduce | flops 6144 | bytes 49152
  315.2 1.3 constant_dynamic-update-slice_fusion.39
  317.5 1.7 collective-permute-start.21
  319.2 1.7 collective-permute-start.22
  321.0 1.4 collective-permute-start.24
  322.5 2.8 collective-permute-start.25
  325.4 1.6 collective-permute-done.25
  327.0 2.3 collective-permute-done.26
  329.6 3.5 %collective-permute-start.27 = (f32[8,6,128]{2,1,0:T(8,128)S(1)}, f32[8,6,128]{2,1,0:T(8,128)S(1)}, u32[]{:S(2)}, u32[]{:S(2)}) collective-permute-start(f32[8,6,128]{2,1,0:T(8,128)S(1)} %fusion.313), channel_id=1, source_target_pairs={{0,24},{8,0},{16,8},{24,16},{1,25},{9,1},{17,9},{25,17},{2,26},{10... | collective-permute-start | bytes 73736 | tf_op jit(solution)/shard_map/ppermute | solution.py:108
  333.2 1.9 collective-permute-done.29
  (516 shorter events, 76.8 us)
Async XLA Ops:
  0.6 6.8 %copy-start.2 = (f32[6,128]{1,0:T(8,128)S(1)}, f32[6,128]{1,0:T(8,128)}, u32[]{:S(2)}) copy-start(f32[6,128]{1,0:T(8,128)} %param.36) | copy-start | bytes 9220
  1.4 6.0 %copy-start.5 = (f32[6,128]{1,0:T(8,128)S(1)}, f32[6,128]{1,0:T(8,128)}, u32[]{:S(2)}) copy-start(f32[6,128]{1,0:T(8,128)} %param.37) | copy-start | bytes 9220
  1.4 6.0 %collective-permute-start = (f32[12,128]{1,0:T(8,128)S(1)}, f32[12,128]{1,0:T(8,128)S(1)}, u32[]{:S(2)}, u32[]{:S(2)}) collective-permute-start(f32[12,128]{1,0:T(8,128)S(1)} %pad_maximum_fusion.4), channel_id=1, source_target_pairs={{0,7},{1,0},{2,1},{3,2},{4,3},{5,4},{6,5},{7,6},{8,15},{9,8},{10,9... | collective-permute-start | bytes 18440 | tf_op jit(solution)/shard_map/ppermute | solution.py:108
  4.8 5.0 %collective-permute-start.1 = (f32[12,128]{1,0:T(8,128)S(1)}, f32[12,128]{1,0:T(8,128)S(1)}, u32[]{:S(2)}, u32[]{:S(2)}) collective-permute-start(f32[12,128]{1,0:T(8,128)S(1)} %pad_maximum_fusion.4), channel_id=1, source_target_pairs={{0,6},{1,7},{2,0},{3,1},{4,2},{5,3},{6,4},{7,5},{8,14},{9,15},{10,... | collective-permute-start | bytes 18440 | tf_op jit(solution)/shard_map/ppermute | solution.py:108
  5.4 4.4 %collective-permute-start.2 = (f32[12,128]{1,0:T(8,128)S(1)}, f32[12,128]{1,0:T(8,128)S(1)}, u32[]{:S(2)}, u32[]{:S(2)}) collective-permute-start(f32[12,128]{1,0:T(8,128)S(1)} %pad_maximum_fusion.4), channel_id=1, source_target_pairs={{0,5},{1,6},{2,7},{3,0},{4,1},{5,2},{6,3},{7,4},{8,13},{9,14},{10,... | collective-permute-start | bytes 18440 | tf_op jit(solution)/shard_map/ppermute | solution.py:108
  5.7 4.2 %collective-permute-start.3 = (f32[12,128]{1,0:T(8,128)S(1)}, f32[12,128]{1,0:T(8,128)S(1)}, u32[]{:S(2)}, u32[]{:S(2)}) collective-permute-start(f32[12,128]{1,0:T(8,128)S(1)} %pad_maximum_fusion.4), channel_id=1, source_target_pairs={{0,4},{1,5},{2,6},{3,7},{4,0},{5,1},{6,2},{7,3},{8,12},{9,13},{10,... | collective-permute-start | bytes 18440 | tf_op jit(solution)/shard_map/ppermute | solution.py:108
  7.2 3.1 collective-permute-start.4
  7.4 4.9 %collective-permute-start.5 = (f32[12,128]{1,0:T(8,128)S(1)}, f32[12,128]{1,0:T(8,128)S(1)}, u32[]{:S(2)}, u32[]{:S(2)}) collective-permute-start(f32[12,128]{1,0:T(8,128)S(1)} %pad_maximum_fusion.4), channel_id=1, source_target_pairs={{0,2},{1,3},{2,4},{3,5},{4,6},{5,7},{6,0},{7,1},{8,10},{9,11},{10,... | collective-permute-start | bytes 18440 | tf_op jit(solution)/shard_map/ppermute | solution.py:108
  9.8 4.0 %collective-permute-start.6 = (f32[12,128]{1,0:T(8,128)S(1)}, f32[12,128]{1,0:T(8,128)S(1)}, u32[]{:S(2)}, u32[]{:S(2)}) collective-permute-start(f32[12,128]{1,0:T(8,128)S(1)} %pad_maximum_fusion.4), channel_id=1, source_target_pairs={{0,1},{1,2},{2,3},{3,4},{4,5},{5,6},{6,7},{7,0},{8,9},{9,10},{10,1... | collective-permute-start | bytes 18440 | tf_op jit(solution)/shard_map/ppermute | solution.py:108
  13.9 7.4 %collective-permute-start.7 = (f32[8,12,128]{2,1,0:T(8,128)S(1)}, f32[8,12,128]{2,1,0:T(8,128)S(1)}, u32[]{:S(2)}, u32[]{:S(2)}) collective-permute-start(f32[8,12,128]{2,1,0:T(8,128)S(1)} %get-tuple-element.542), channel_id=1, source_target_pairs={{0,24},{8,0},{16,8},{24,16},{1,25},{9,1},{17,9},{25,17},{2,26},{10... | collective-permute-start | bytes 147464 | tf_op jit(solution)/shard_map/ppermute | solution.py:108
  20.3 5.2 %collective-permute-start.8 = (f32[8,12,128]{2,1,0:T(8,128)S(1)}, f32[8,12,128]{2,1,0:T(8,128)S(1)}, u32[]{:S(2)}, u32[]{:S(2)}) collective-permute-start(f32[8,12,128]{2,1,0:T(8,128)S(1)} %get-tuple-element.542), channel_id=1, source_target_pairs={{0,16},{8,24},{16,0},{24,8},{1,17},{9,25},{17,1},{25,9},{2,18},{10... | collective-permute-start | bytes 147464 | tf_op jit(solution)/shard_map/ppermute | solution.py:108
  20.3 6.1 %collective-permute-start.9 = (f32[8,12,128]{2,1,0:T(8,128)S(1)}, f32[8,12,128]{2,1,0:T(8,128)S(1)}, u32[]{:S(2)}, u32[]{:S(2)}) collective-permute-start(f32[8,12,128]{2,1,0:T(8,128)S(1)} %get-tuple-element.542), channel_id=1, source_target_pairs={{0,8},{8,16},{16,24},{24,0},{1,9},{9,17},{17,25},{25,1},{2,10},{10... | collective-permute-start | bytes 147464 | tf_op jit(solution)/shard_map/ppermute | solution.py:108
  159.9 6.0 %collective-permute-start.10 = (f32[6,128]{1,0:T(8,128)S(1)}, f32[6,128]{1,0:T(8,128)S(1)}, u32[]{:S(2)}, u32[]{:S(2)}) collective-permute-start(f32[6,128]{1,0:T(8,128)S(1)} %get-tuple-element.515), channel_id=1, source_target_pairs={{0,7},{1,0},{2,1},{3,2},{4,3},{5,4},{6,5},{7,6},{8,15},{9,8},{10,9... | collective-permute-start | bytes 9224 | tf_op jit(solution)/shard_map/ppermute | solution.py:108
  161.0 7.7 %collective-permute-start.11 = (f32[6,128]{1,0:T(8,128)S(1)}, f32[6,128]{1,0:T(8,128)S(1)}, u32[]{:S(2)}, u32[]{:S(2)}) collective-permute-start(f32[6,128]{1,0:T(8,128)S(1)} %get-tuple-element.515), channel_id=1, source_target_pairs={{0,6},{1,7},{2,0},{3,1},{4,2},{5,3},{6,4},{7,5},{8,14},{9,15},{10,... | collective-permute-start | bytes 9224 | tf_op jit(solution)/shard_map/ppermute | solution.py:108
  162.7 6.1 %collective-permute-start.12 = (f32[6,128]{1,0:T(8,128)S(1)}, f32[6,128]{1,0:T(8,128)S(1)}, u32[]{:S(2)}, u32[]{:S(2)}) collective-permute-start(f32[6,128]{1,0:T(8,128)S(1)} %get-tuple-element.515), channel_id=1, source_target_pairs={{0,5},{1,6},{2,7},{3,0},{4,1},{5,2},{6,3},{7,4},{8,13},{9,14},{10,... | collective-permute-start | bytes 9224 | tf_op jit(solution)/shard_map/ppermute | solution.py:108
  164.4 4.4 %collective-permute-start.13 = (f32[6,128]{1,0:T(8,128)S(1)}, f32[6,128]{1,0:T(8,128)S(1)}, u32[]{:S(2)}, u32[]{:S(2)}) collective-permute-start(f32[6,128]{1,0:T(8,128)S(1)} %get-tuple-element.515), channel_id=1, source_target_pairs={{0,4},{1,5},{2,6},{3,7},{4,0},{5,1},{6,2},{7,3},{8,12},{9,13},{10,... | collective-permute-start | bytes 9224 | tf_op jit(solution)/shard_map/ppermute | solution.py:108
  164.5 4.3 %collective-permute-start.14 = (f32[6,128]{1,0:T(8,128)S(1)}, f32[6,128]{1,0:T(8,128)S(1)}, u32[]{:S(2)}, u32[]{:S(2)}) collective-permute-start(f32[6,128]{1,0:T(8,128)S(1)} %get-tuple-element.515), channel_id=1, source_target_pairs={{0,3},{1,4},{2,5},{3,6},{4,7},{5,0},{6,1},{7,2},{8,11},{9,12},{10,... | collective-permute-start | bytes 9224 | tf_op jit(solution)/shard_map/ppermute | solution.py:108
  166.0 4.5 %collective-permute-start.15 = (f32[6,128]{1,0:T(8,128)S(1)}, f32[6,128]{1,0:T(8,128)S(1)}, u32[]{:S(2)}, u32[]{:S(2)}) collective-permute-start(f32[6,128]{1,0:T(8,128)S(1)} %get-tuple-element.515), channel_id=1, source_target_pairs={{0,2},{1,3},{2,4},{3,5},{4,6},{5,7},{6,0},{7,1},{8,10},{9,11},{10,... | collective-permute-start | bytes 9224 | tf_op jit(solution)/shard_map/ppermute | solution.py:108
  168.8 3.9 %collective-permute-start.16 = (f32[6,128]{1,0:T(8,128)S(1)}, f32[6,128]{1,0:T(8,128)S(1)}, u32[]{:S(2)}, u32[]{:S(2)}) collective-permute-start(f32[6,128]{1,0:T(8,128)S(1)} %get-tuple-element.515), channel_id=1, source_target_pairs={{0,1},{1,2},{2,3},{3,4},{4,5},{5,6},{6,7},{7,0},{8,9},{9,10},{10,1... | collective-permute-start | bytes 9224 | tf_op jit(solution)/shard_map/ppermute | solution.py:108
  172.8 5.8 %collective-permute-start.19 = (f32[8,6,128]{2,1,0:T(8,128)S(1)}, f32[8,6,128]{2,1,0:T(8,128)S(1)}, u32[]{:S(2)}, u32[]{:S(2)}) collective-permute-start(f32[8,6,128]{2,1,0:T(8,128)S(1)} %fusion.314), channel_id=1, source_target_pairs={{0,8},{8,16},{16,24},{24,0},{1,9},{9,17},{17,25},{25,1},{2,10},{10... | collective-permute-start | bytes 73736 | tf_op jit(solution)/shard_map/ppermute | solution.py:108
  172.8 5.7 %collective-permute-start.18 = (f32[8,6,128]{2,1,0:T(8,128)S(1)}, f32[8,6,128]{2,1,0:T(8,128)S(1)}, u32[]{:S(2)}, u32[]{:S(2)}) collective-permute-start(f32[8,6,128]{2,1,0:T(8,128)S(1)} %fusion.314), channel_id=1, source_target_pairs={{0,16},{8,24},{16,0},{24,8},{1,17},{9,25},{17,1},{25,9},{2,18},{10... | collective-permute-start | bytes 73736 | tf_op jit(solution)/shard_map/ppermute | solution.py:108
  173.1 6.0 %collective-permute-start.17 = (f32[8,6,128]{2,1,0:T(8,128)S(1)}, f32[8,6,128]{2,1,0:T(8,128)S(1)}, u32[]{:S(2)}, u32[]{:S(2)}) collective-permute-start(f32[8,6,128]{2,1,0:T(8,128)S(1)} %fusion.314), channel_id=1, source_target_pairs={{0,24},{8,0},{16,8},{24,16},{1,25},{9,1},{17,9},{25,17},{2,26},{10... | collective-permute-start | bytes 73736 | tf_op jit(solution)/shard_map/ppermute | solution.py:108
  316.4 6.0 %collective-permute-start.20 = (f32[6,128]{1,0:T(8,128)S(1)}, f32[6,128]{1,0:T(8,128)S(1)}, u32[]{:S(2)}, u32[]{:S(2)}) collective-permute-start(f32[6,128]{1,0:T(8,128)S(1)} %get-tuple-element.501), channel_id=1, source_target_pairs={{0,7},{1,0},{2,1},{3,2},{4,3},{5,4},{6,5},{7,6},{8,15},{9,8},{10,9... | collective-permute-start | bytes 9224 | tf_op jit(solution)/shard_map/ppermute | solution.py:108
  317.5 7.7 %collective-permute-start.21 = (f32[6,128]{1,0:T(8,128)S(1)}, f32[6,128]{1,0:T(8,128)S(1)}, u32[]{:S(2)}, u32[]{:S(2)}) collective-permute-start(f32[6,128]{1,0:T(8,128)S(1)} %get-tuple-element.501), channel_id=1, source_target_pairs={{0,6},{1,7},{2,0},{3,1},{4,2},{5,3},{6,4},{7,5},{8,14},{9,15},{10,... | collective-permute-start | bytes 9224 | tf_op jit(solution)/shard_map/ppermute | solution.py:108
  319.2 6.1 %collective-permute-start.22 = (f32[6,128]{1,0:T(8,128)S(1)}, f32[6,128]{1,0:T(8,128)S(1)}, u32[]{:S(2)}, u32[]{:S(2)}) collective-permute-start(f32[6,128]{1,0:T(8,128)S(1)} %get-tuple-element.501), channel_id=1, source_target_pairs={{0,5},{1,6},{2,7},{3,0},{4,1},{5,2},{6,3},{7,4},{8,13},{9,14},{10,... | collective-permute-start | bytes 9224 | tf_op jit(solution)/shard_map/ppermute | solution.py:108
  320.9 4.4 %collective-permute-start.23 = (f32[6,128]{1,0:T(8,128)S(1)}, f32[6,128]{1,0:T(8,128)S(1)}, u32[]{:S(2)}, u32[]{:S(2)}) collective-permute-start(f32[6,128]{1,0:T(8,128)S(1)} %get-tuple-element.501), channel_id=1, source_target_pairs={{0,4},{1,5},{2,6},{3,7},{4,0},{5,1},{6,2},{7,3},{8,12},{9,13},{10,... | collective-permute-start | bytes 9224 | tf_op jit(solution)/shard_map/ppermute | solution.py:108
  321.0 4.3 %collective-permute-start.24 = (f32[6,128]{1,0:T(8,128)S(1)}, f32[6,128]{1,0:T(8,128)S(1)}, u32[]{:S(2)}, u32[]{:S(2)}) collective-permute-start(f32[6,128]{1,0:T(8,128)S(1)} %get-tuple-element.501), channel_id=1, source_target_pairs={{0,3},{1,4},{2,5},{3,6},{4,7},{5,0},{6,1},{7,2},{8,11},{9,12},{10,... | collective-permute-start | bytes 9224 | tf_op jit(solution)/shard_map/ppermute | solution.py:108
  322.5 4.5 %collective-permute-start.25 = (f32[6,128]{1,0:T(8,128)S(1)}, f32[6,128]{1,0:T(8,128)S(1)}, u32[]{:S(2)}, u32[]{:S(2)}) collective-permute-start(f32[6,128]{1,0:T(8,128)S(1)} %get-tuple-element.501), channel_id=1, source_target_pairs={{0,2},{1,3},{2,4},{3,5},{4,6},{5,7},{6,0},{7,1},{8,10},{9,11},{10,... | collective-permute-start | bytes 9224 | tf_op jit(solution)/shard_map/ppermute | solution.py:108
  325.3 3.9 %collective-permute-start.26 = (f32[6,128]{1,0:T(8,128)S(1)}, f32[6,128]{1,0:T(8,128)S(1)}, u32[]{:S(2)}, u32[]{:S(2)}) collective-permute-start(f32[6,128]{1,0:T(8,128)S(1)} %get-tuple-element.501), channel_id=1, source_target_pairs={{0,1},{1,2},{2,3},{3,4},{4,5},{5,6},{6,7},{7,0},{8,9},{9,10},{10,1... | collective-permute-start | bytes 9224 | tf_op jit(solution)/shard_map/ppermute | solution.py:108
  329.3 5.8 %collective-permute-start.29 = (f32[8,6,128]{2,1,0:T(8,128)S(1)}, f32[8,6,128]{2,1,0:T(8,128)S(1)}, u32[]{:S(2)}, u32[]{:S(2)}) collective-permute-start(f32[8,6,128]{2,1,0:T(8,128)S(1)} %fusion.313), channel_id=1, source_target_pairs={{0,8},{8,16},{16,24},{24,0},{1,9},{9,17},{17,25},{25,1},{2,10},{10... | collective-permute-start | bytes 73736 | tf_op jit(solution)/shard_map/ppermute | solution.py:108
  329.3 5.7 %collective-permute-start.28 = (f32[8,6,128]{2,1,0:T(8,128)S(1)}, f32[8,6,128]{2,1,0:T(8,128)S(1)}, u32[]{:S(2)}, u32[]{:S(2)}) collective-permute-start(f32[8,6,128]{2,1,0:T(8,128)S(1)} %fusion.313), channel_id=1, source_target_pairs={{0,16},{8,24},{16,0},{24,8},{1,17},{9,25},{17,1},{25,9},{2,18},{10... | collective-permute-start | bytes 73736 | tf_op jit(solution)/shard_map/ppermute | solution.py:108
  329.6 6.0 %collective-permute-start.27 = (f32[8,6,128]{2,1,0:T(8,128)S(1)}, f32[8,6,128]{2,1,0:T(8,128)S(1)}, u32[]{:S(2)}, u32[]{:S(2)}) collective-permute-start(f32[8,6,128]{2,1,0:T(8,128)S(1)} %fusion.313), channel_id=1, source_target_pairs={{0,24},{8,0},{16,8},{24,16},{1,25},{9,1},{17,9},{25,17},{2,26},{10... | collective-permute-start | bytes 73736 | tf_op jit(solution)/shard_map/ppermute | solution.py:108
  (10 other events, 7.0 us)

commit v3 on v1

--- a/solution.py
+++ b/solution.py
@@ -102,8 +102,9 @@
     used = tile_count[0, 0]
 
     def everywhere(values):
-        gathered = lax.all_gather(values, ("row", "col"), axis=0, tiled=False)
-        return gathered.reshape((row_devices, col_devices) + values.shape)
+        copies = jnp.broadcast_to(values, (row_devices * col_devices,) + values.shape)
+        arrived = lax.all_to_all(copies, ("row", "col"), 0, 0, tiled=True)
+        return arrived.reshape((row_devices, col_devices) + values.shape)
 
     def mean_of(values):
         return jnp.sum(values) / total_entries

time: 399 us -> 321 us (0.80)
  other arithmetic: 100 us -> 26.1 us
  loops' own time: 65.7 us -> 10.7 us
  blocking collectives: 216 us -> 247 us
  waiting for transfers between devices: 0 us -> 15.4 us
  starting transfers between devices: 0 us -> 9.86 us
  local copies, waits for them, and re-layouts: 14.9 us -> 6.91 us
    unnamed x4, blocking collectives: 98.9 us -> 237 us
    all_gather x3 -> x0, blocking collectives: 117 us -> none  [everywhere(): gathered = lax.all_gather(values, ('row', 'col'), axis=0, tiled=False)]
    another operation x2, loops' own time: 65.7 us -> 10.7 us  [apply_hessian(): lax.fori_loop(0, used, visit, (jnp.zeros_like(row_vectors), jnp.zeros_lik...]
    another operation x28 -> x4, other arithmetic: 20.7 us -> 2.96 us
    all_to_all x0 -> x2, waiting for transfers between devices: none -> 15.4 us  [everywhere(): arrived = lax.all_to_all(copies, ('row', 'col'), 0, 0, tiled=True)]
    scatter-add x14 -> x2, other arithmetic: 17.1 us -> 2.44 us  [visit(): row_total.at[left].add(left_out)]
    reduce_sum x32 -> x8, other arithmetic: 13.8 us -> 3.18 us  [pair_energy(): along_right = jnp.sum(direction * right_axis, axis=0)]
    all_to_all x0 -> x1, blocking collectives: none -> 9.93 us  [everywhere(): arrived = lax.all_to_all(copies, ('row', 'col'), 0, 0, tiled=True)]
  transfers between devices with their start and end apart: 0 -> 2, of which waited for: 0 -> 2; matrix products, arithmetic and copies ran while one was open for 0% -> 0% of each run, Pallas kernels for 0% -> 0%
where the time goes in v3:
time: 321 us; the launch traced here: 320 us
  blocking collectives  247 us (77%)
  other arithmetic  26.1 us (8%)
  waiting for transfers between devices  15.4 us (5%)
  loops' own time  10.7 us (3%)
  starting transfers between devices  9.86 us (3%)
  local copies, waits for them, and re-layouts  6.91 us (2%)
  between operations  4.43 us (1%)
    unnamed x4, blocking collectives  237 us
    all_to_all x2, waiting for transfers between devices, everywhere(): arrived = lax.all_to_all(copies, ('row', 'col'), 0, 0, tiled=True)  15.4 us
    another operation x2, loops' own time, apply_hessian(): lax.fori_loop(0, used, visit, (jnp.zeros_like(row_vectors), jnp.zeros_lik...  10.7 us
    all_to_all x1, blocking collectives, everywhere(): arrived = lax.all_to_all(copies, ('row', 'col'), 0, 0, tiled=True)  9.93 us
    all_to_all x2, starting transfers between devices, everywhere(): arrived = lax.all_to_all(copies, ('row', 'col'), 0, 0, tiled=True)  9.86 us
  transfers between devices with their start and end apart: 2, of which 2 were waited for; matrix products, arithmetic and copies ran while one was open for 0% of the time, Pallas kernels for 0%

profile of v3, /device:TPU:0, one launch (start us, length us, event | category | flops | bytes accessed | tf_op | source)
XLA Modules:
  0.0 320.0 jit_solution(6726687713901177907)
XLA Ops:
  0.6 0.7 pad_maximum_fusion.4
  1.3 0.7 broadcast_in_dim.166
  2.1 7.3 %all-to-all-start = ((f32[32,12,128]{2,1,0:T(8,128)}), f32[32,12,128]{2,1,0:T(8,128)S(1)}, u32[]{:S(2)}, u32[]{:S(2)}) async-start(f32[32,12,128]{2,1,0:T(8,128)} %broadcast_in_dim.166), calls=%async_computation | async-start | bytes 524288 | tf_op jit(solution)/shard_map/all_to_all | solution.py:106
  9.4 0.7 copy-done.5
  10.1 0.7 copy-done.8
  11.4 0.6 dynamic-slice.54
  12.1 0.7 copy-done.4
  12.8 7.2 %all-to-all-done = f32[32,12,128]{2,1,0:T(8,128)S(1)} async-done(((f32[32,12,128]{2,1,0:T(8,128)}), f32[32,12,128]{2,1,0:T(8,128)S(1)}, u32[]{:S(2)}, u32[]{:S(2)}) %all-to-all-start) | async-done | bytes 196640 | tf_op jit(solution)/shard_map/all_to_all | solution.py:106
  20.0 0.6 multiply_reduce_fusion.39
  25.5 11.9 %while.30 = (s32[]{:T(128)}, f32[8,6,128]{2,1,0:T(8,128)S(1)}, f32[4,6,128]{2,1,0:T(8,128)S(1)}, s32[]{:T(128)}, s32[8,5]{1,0:T(8,128)S(1)}, /*index=5*/f32[8,6,...) while((s32[]{:T(128)}, f32[8,6,128]{2,1,0:T(8,128)S(1)}, ...), condition=%wide.region_56.61_spmd.clone, body=%wide.region_25.60_spmd.sunk.clone.sunk | while | flops 15416883 | bytes 7267763 | solution.py:138
  31.3 0.7 fusion.374
  34.1 0.7 and_reduce_fusion.9
  34.8 0.7 and_reduce_fusion.8
  35.5 1.2 fusion.380
  37.4 53.6 %all-reduce.21 = f32[8,6,128]{2,1,0:T(8,128)S(1)} all-reduce(f32[8,6,128]{2,1,0:T(8,128)S(1)} %get-tuple-element.198), channel_id=2, replica_groups=mesh['row'=4,'col'=8] {'col'}, use_global_device_ids=true, to_apply=%region_57.62.clone | all-reduce | flops 6144 | bytes 49152
  91.0 63.8 %all-reduce.22 = f32[4,6,128]{2,1,0:T(8,128)S(1)} all-reduce(f32[4,6,128]{2,1,0:T(8,128)S(1)} %get-tuple-element.199), channel_id=3, replica_groups=mesh['row'=4,'col'=8] {'row'}, use_global_device_ids=true, to_apply=%region_58.63.clone | all-reduce | flops 3072 | bytes 24576
  154.8 1.3 bitcast_add_fusion.4
  156.0 0.6 broadcast_in_dim.177
  156.7 2.6 all-to-all-start.1
  159.2 8.2 %all-to-all-done.1 = f32[32,6,128]{2,1,0:T(8,128)S(1)} async-done(((f32[32,6,128]{2,1,0:T(8,128)}), f32[32,6,128]{2,1,0:T(8,128)S(1)}, u32[]{:S(2)}, u32[]{:S(2)}) %all-to-all-start.1) | async-done | bytes 98336 | tf_op jit(solution)/shard_map/all_to_all | solution.py:106
  167.5 0.6 multiply_reduce_fusion.38
  168.8 0.6 multiply_reduce_fusion.37
  173.1 12.4 %while.31 = (s32[]{:T(128)}, f32[8,6,128]{2,1,0:T(8,128)S(1)}, f32[4,6,128]{2,1,0:T(8,128)S(1)}, s32[]{:T(128)}, s32[8,5]{1,0:T(8,128)S(1)}, /*index=5*/f32[8,6,...) while((s32[]{:T(128)}, f32[8,6,128]{2,1,0:T(8,128)S(1)}, ...), condition=%wide.region_115.120_spmd.clone, body=%wide.region_84.119_spmd.sunk.clone.sunk | while | flops 15416883 | bytes 7267763 | solution.py:138
  179.3 0.7 fusion.385
  182.1 0.7 and_reduce_fusion.11
  182.9 0.8 and_reduce_fusion.10
  183.6 1.2 fusion.391
  185.5 54.4 %all-reduce.23 = f32[8,6,128]{2,1,0:T(8,128)S(1)} all-reduce(f32[8,6,128]{2,1,0:T(8,128)S(1)} %get-tuple-element.205), channel_id=4, replica_groups=mesh['row'=4,'col'=8] {'col'}, use_global_device_ids=true, to_apply=%region_116.121.clone | all-reduce | flops 6144 | bytes 49152
  239.9 65.0 %all-reduce.24 = f32[4,6,128]{2,1,0:T(8,128)S(1)} all-reduce(f32[4,6,128]{2,1,0:T(8,128)S(1)} %get-tuple-element.206), channel_id=5, replica_groups=mesh['row'=4,'col'=8] {'row'}, use_global_device_ids=true, to_apply=%region_117.122.clone | all-reduce | flops 3072 | bytes 24576
  304.9 1.3 bitcast_subtract_fusion
  306.2 9.9 %all_to_all.15 = f32[32,6,128]{2,1,0:T(8,128)S(1)} all-to-all(f32[32,6,128]{2,1,0:T(8,128)S(1)} %broadcast_in_dim.272), channel_id=1, replica_groups=mesh['row'=4,'col'=8] {'row','col'}, dimensions={0} | all-to-all | bytes 196608 | tf_op jit(solution)/shard_map/all_to_all | solution.py:106
  316.1 0.6 multiply_reduce_fusion.36
  (163 shorter events, 16.4 us)
Async XLA Ops:
  2.1 17.9 %all-to-all-start = ((f32[32,12,128]{2,1,0:T(8,128)}), f32[32,12,128]{2,1,0:T(8,128)S(1)}, u32[]{:S(2)}, u32[]{:S(2)}) async-start(f32[32,12,128]{2,1,0:T(8,128)} %broadcast_in_dim.166), calls=%async_computation | async-start | bytes 524288 | tf_op jit(solution)/shard_map/all_to_all | solution.py:106
  9.4 0.7 copy-start.5
  10.1 0.7 copy-start.8
  10.8 0.7 copy-start.7
  12.1 0.7 copy-start.4
  21.4 3.3 %copy-start.1 = (f32[8,12,128]{2,1,0:T(8,128)}, f32[8,12,128]{2,1,0:T(8,128)S(1)}, u32[]{:S(2)}) copy-start(f32[8,12,128]{2,1,0:T(8,128)S(1)} %dynamic-slice_bitcast_fusion) | copy-start | bytes 147460
  21.4 3.3 %copy-start = (f32[4,12,128]{2,1,0:T(8,128)}, f32[4,12,128]{2,1,0:T(8,128)S(1)}, u32[]{:S(2)}) copy-start(f32[4,12,128]{2,1,0:T(8,128)S(1)} %dynamic-slice_bitcast_fusion.2) | copy-start | bytes 73732
  24.7 0.7 copy-start.3
  24.7 0.7 copy-start.6
  24.7 0.8 slice-start.1
  24.7 0.7 slice-start
  24.8 0.7 copy-start.2
  156.7 10.8 %all-to-all-start.1 = ((f32[32,6,128]{2,1,0:T(8,128)}), f32[32,6,128]{2,1,0:T(8,128)S(1)}, u32[]{:S(2)}, u32[]{:S(2)}) async-start(f32[32,6,128]{2,1,0:T(8,128)} %broadcast_in_dim.177), calls=%async_computation.1 | async-start | bytes 262144 | tf_op jit(solution)/shard_map/all_to_all | solution.py:106

commit v4 on v1

v4 whole, which is shorter than its diff:
```python
import functools
import math

import jax
import jax.numpy as jnp
from jax import lax
from jax.experimental import pallas as pl
from jax.experimental.pallas import tpu as pltpu
from jax.sharding import PartitionSpec as P

chi_shape = 0.8
chi_energy = (math.sqrt(5.0) - 1.0) / (math.sqrt(5.0) + 1.0)
well_depth = 0.005
cutoff_sq = 20.25
norm_eps = 1e-06

SUB = 8
FRAME = 8
LIST_ROW = 14
ROWS = 16
VMEM_LIMIT = 48 * 1024 * 1024


def dot3(a, b):
    return a[0] * b[0] + a[1] * b[1] + a[2] * b[2]


def cross3(a, b):
    return (
        a[1] * b[2] - a[2] * b[1],
        a[2] * b[0] - a[0] * b[2],
        a[0] * b[1] - a[1] * b[0],
    )


def bracket(chi, scaled, factor, p, a, b, eps, da, db, dc):
    f = factor * (a - scaled * b)
    g = factor * (b - scaled * a)
    y = p * (a * f + b * g)
    bent = chi * dc
    da_bent = da - bent * g
    db_bent = db - bent * f
    df = factor * (da_bent - scaled * db_bent)
    dg = factor * (db_bent - scaled * da_bent)
    half_dy = p * (f * da_bent + g * db - eps * y)
    return f, g, y, df, dg, half_dy


def pair_tangent(d, ui, uj, dd, dui, duj, lift):
    r_sq = dot3(d, d) + lift
    a = dot3(d, ui)
    b = dot3(d, uj)
    c = dot3(ui, uj)
    eps = dot3(d, dd)
    da = dot3(dd, ui) + dot3(d, dui)
    db = dot3(dd, uj) + dot3(d, duj)
    dc = dot3(dui, uj) + dot3(ui, duj)
    r_inv = lax.rsqrt(r_sq)
    p = r_inv * r_inv
    r = r_sq * r_inv
    x = jnp.maximum(1.0 - r_sq * (1.0 / cutoff_sq), 0.0)
    c_shape = chi_shape * c
    c_energy = chi_energy * c
    e1 = lax.rsqrt(1.0 - c_shape * c_shape)
    q = e1 * e1
    q2 = 1.0 / (1.0 - c_energy * c_energy)
    f, g, y, df, dg, hdy = bracket(chi_shape, c_shape, q, p, a, b, eps, da, db, dc)
    f2, g2, y2, df2, dg2, hdy2 = bracket(chi_energy, c_energy, q2, p, a, b, eps, da, db, dc)
    sigma = lax.rsqrt(1.0 - chi_shape * y)
    sigma_sq = sigma * sigma
    sigma_cu = sigma_sq * sigma
    psi = 1.0 - chi_energy * y2
    s = 1.0 / (r - sigma + 1.0)
    s_sq = s * s
    s6 = s_sq * s_sq * s_sq
    t0 = s6 * (s6 - 1.0)
    t1 = s6 * s * (6.0 - 12.0 * s6)
    t2 = s6 * s_sq * (156.0 * s6 - 42.0)
    ke = (4.0 * well_depth) * e1
    kx = ke * x
    vrr = kx * (6.0 / cutoff_sq**2)
    kxx = kx * x
    vr = kxx * (-3.0 / cutoff_sq)
    v = kxx * x
    psi_sq = psi * psi
    psi_sq_t0 = psi_sq * t0
    v_psi = v * psi
    v_psi_t0 = v_psi * t0
    v_psi_t1 = v_psi * t1
    v_psi_sq = v_psi * psi
    slope = v_psi * psi * t1
    pull = (-chi_shape) * p * sigma_cu
    h1 = pull * slope
    push = (-4.0 * chi_energy) * p
    h2 = push * v_psi_t0
    u_a = h1 * f + h2 * f2
    u_b = h1 * g + h2 * g2
    kc = chi_shape * c_shape * q
    u = v * psi_sq_t0
    fg = chi_shape * f * g
    fg2 = chi_energy * f2 * g2
    u_c = u * kc - (h1 * fg + h2 * fg2)
    u_r = r_inv * slope + 2.0 * vr * psi_sq_t0 - (h1 * y + h2 * y2)

    dy = 2.0 * hdy
    dy2 = 2.0 * hdy2
    d_sigma = chi_shape * sigma_cu * hdy
    d_rho = r_inv * eps - d_sigma
    d_psi = (-chi_energy) * dy2
    eps2 = 2.0 * eps
    kc_dc = kc * dc
    dv = v * kc_dc + vr * eps2
    dvr = vr * kc_dc + vrr * eps2
    d_psi2 = 2.0 * d_psi
    d_slope = dv * psi_sq * t1 + v_psi_t1 * d_psi2 + v_psi_sq * t2 * d_rho
    fall = p * eps2
    dh1 = h1 * ((3.0 * chi_shape) * sigma_sq * hdy - fall) + pull * d_slope
    dh2 = push * (dv * psi * t0 + v * d_psi * t0 + v_psi_t1 * d_rho) - h2 * fall
    du_a = dh1 * f + h1 * df + dh2 * f2 + h2 * df2
    du_b = dh1 * g + h1 * dg + dh2 * g2 + h2 * dg2
    d_kc = (chi_shape * chi_shape) * q * (2.0 * q - 1.0) * dc
    d_well = psi * d_psi2 * t0 + psi_sq * t1 * d_rho
    du = dv * psi_sq_t0 + v * d_well
    du_c = (
        du * kc
        + u * d_kc
        - (dh1 * fg + chi_shape * h1 * (df * g + f * dg))
        - (dh2 * fg2 + chi_energy * h2 * (df2 * g2 + f2 * dg2))
    )
    du_r = (
        r_inv * (d_slope - p * eps * slope)
        + 2.0 * (dvr * psi_sq_t0 + vr * d_well)
        - (dh1 * y + h1 * dy + dh2 * y2 + h2 * dy2)
    )
    return a, c, u_r, u_a, u_b, u_c, du_r, du_a, du_b, du_c


def tile_product(count, own, frame, moved, entry_tile, entry_shift, skew_ref):
    member = frame(own, 0).shape[1]

    def wide(row):
        return jnp.broadcast_to(row, (SUB, member))

    xi = [wide(frame(own, k)) for k in range(3)]
    ui = [wide(frame(own, k)) for k in range(3, 6)]
    dxi = [wide(moved(own, k)) for k in range(3)]
    dui = [wide(moved(own, k)) for k in range(3, 6)]
    first_row = (lax.broadcasted_iota(jnp.int32, (SUB, member), 0) == 0).astype(jnp.float32)

    sublane = lax.broadcasted_iota(jnp.int32, (SUB, member), 0)

    def skewed(row):
        block = wide(row)
        for bit in (1, 2, 4):
            block = jnp.where((sublane & bit) > 0, pltpu.roll(block, bit, 1), block)
        return block

    def visit_entry(entry, totals):
        partner = entry_tile(entry)
        shift = entry_shift(entry)
        for k in range(3):
            skew_ref[k] = skewed(frame(partner, k)) + shift[k]
        for k in range(3, 6):
            skew_ref[k] = skewed(frame(partner, k))
        for k in range(6):
            skew_ref[6 + k] = skewed(moved(partner, k))
        return lax.fori_loop(0, member // SUB, functools.partial(visit, entry), totals)

    def visit(entry, block, totals):
        other = [pltpu.roll(skew_ref[k], block * SUB, 1) for k in range(12)]
        d = [other[k] - xi[k] for k in range(3)]
        uj = other[3:6]
        dd = [other[6 + k] - dxi[k] for k in range(3)]
        duj = other[9:12]
        item = entry * (member // SUB) + block
        lift = first_row * jnp.where(item == 0, 2.0 * cutoff_sq, 0.0)
        a, c, u_r, u_a, u_b, u_c, du_r, du_a, du_b, du_c = pair_tangent(d, ui, uj, dd, dui, duj, lift)
        force = [du_r * d[k] + u_r * dd[k] + du_b * uj[k] + u_b * duj[k] for k in range(3)]
        turn = [du_a * d[k] + u_a * dd[k] + du_c * uj[k] + u_c * duj[k] for k in range(3)]
        news = force + turn + [du_a, u_a, u_a * a + u_c * c]
        return tuple(total + new for total, new in zip(totals, news))

    zero = jnp.zeros((SUB, member), jnp.float32)
    totals = lax.fori_loop(0, count, visit_entry, (zero,) * 9)
    sums = [jnp.sum(total, axis=0, keepdims=True) for total in totals]
    u = [row[:1] for row in ui]
    t = [row[:1] for row in dui]
    force = [-(sums[k] + u[k] * sums[6] + t[k] * sums[7]) for k in range(3)]
    turn = cross3(u, [sums[3 + k] - t[k] * sums[8] for k in range(3)])
    return force + list(cross3(turn, u))


def spread(rows, out_ref):
    member = rows[0].shape[1]
    fill = [jnp.zeros((1, member), jnp.float32)] * (SUB - len(rows))
    block = jnp.concatenate(rows + fill, axis=0)
    out_ref[...] = jnp.broadcast_to(block[None], out_ref.shape)


def pack_kernel(config_ref, start_ref, list_ref, out_ref):
    u = [config_ref[k : k + 1, :] for k in range(3, 6)]
    w = [start_ref[k : k + 1, :] for k in range(3, 6)]
    t = cross3(w, u)
    zero = jnp.zeros_like(u[0])
    block = jnp.concatenate(
        [start_ref[0:3, :], t[0], t[1], t[2], dot3(w, u), zero, config_ref[...], list_ref[...], zero], axis=0
    )
    out_ref[...] = jnp.broadcast_to(block[None], out_ref.shape)


def first_kernel(rows, cols, period, all_ref, out_ref, tile_ref, shift_ref, count_ref, skew_ref, code_ref, code_smem, sem):
    member = all_ref.shape[2]
    row_id = lax.axis_index("row")
    col_id = lax.axis_index("col")
    own = row_id * cols + col_id
    slots = SUB

    def field(line, at):
        return line if at == 0 else pltpu.roll(line, member - at * slots, 1)

    def encode(line, partner, side):
        offset = (field(line, 2) * 9.0 + field(line, 3) * 3.0 + field(line, 4)) * side + 13.0
        return partner * 27.0 + offset

    row_f = row_id.astype(jnp.float32)
    col_f = col_id.astype(jnp.float32)
    for col in range(cols):
        line = all_ref[row_id * cols + col, LIST_ROW : LIST_ROW + 1, :]
        code = encode(line, field(line, 1) * float(cols) + float(col), 1.0)
        code_ref[col : col + 1, :] = jnp.where(line == col_f, code, -1.0).astype(jnp.int32)
    for row in range(rows):
        line = all_ref[row * cols + col_id, LIST_ROW : LIST_ROW + 1, :]
        code = encode(line, float(row * cols) + line, -1.0)
        hit = (field(line, 1) == row_f) & (line >= 0.0)
        code_ref[cols + row : cols + row + 1, :] = jnp.where(hit, code, -1.0).astype(jnp.int32)
    copy = pltpu.make_async_copy(code_ref, code_smem, sem)
    copy.start()
    copy.wait()

    tile_ref[0] = own
    for k in range(3):
        shift_ref[k] = 0.0

    def gather(at, count):
        code = code_smem[at // slots, at % slots]

        @pl.when(code >= 0)
        def _():
            offset = code % 27
            tile_ref[count] = code // 27
            shift_ref[count * 3] = (offset // 9 - 1).astype(jnp.float32) * period[0]
            shift_ref[count * 3 + 1] = (offset // 3 % 3 - 1).astype(jnp.float32) * period[1]
            shift_ref[count * 3 + 2] = (offset % 3 - 1).astype(jnp.float32) * period[2]

        return count + (code >= 0).astype(jnp.int32)

    count = lax.fori_loop(0, (rows + cols) * slots, gather, jnp.int32(1))
    count_ref[0] = count
    product = tile_product(
        count,
        own,
        lambda tile, k: all_ref[tile, FRAME + k : FRAME + k + 1, :],
        lambda tile, k: all_ref[tile, k : k + 1, :],
        lambda entry: tile_ref[entry],
        lambda entry: [shift_ref[entry * 3 + k] for k in range(3)],
        skew_ref,
    )
    spread(product, out_ref)


def whole_sum(left_ref, right_ref):
    total = jnp.sum(left_ref[...] * right_ref[...], axis=0)
    return jnp.sum(jnp.sum(total, axis=0, keepdims=True), axis=1, keepdims=True)


def second_kernel(
    cols, total_entries, tile_ref, shift_ref, count_ref, all_ref, image_ref, out_ref, second_ref, scalar_ref, skew_ref, basis_ref
):
    own = lax.axis_index("row") * cols + lax.axis_index("col")
    member = all_ref.shape[2]
    basis_ref[...] = all_ref[:, 0:SUB, :]
    norm_sq = whole_sum(basis_ref, basis_ref) / total_entries + norm_eps
    alpha = whole_sum(basis_ref, image_ref) / total_entries / norm_sq
    second_ref[...] = image_ref[...] - alpha * basis_ref[...]
    beta = jnp.sqrt(whole_sum(second_ref, second_ref) / total_entries / norm_sq + norm_eps)
    scale = lax.rsqrt(norm_sq) / beta
    product = tile_product(
        count_ref[0],
        own,
        lambda tile, k: all_ref[tile, FRAME + k : FRAME + k + 1, :],
        lambda tile, k: second_ref[tile, k : k + 1, :],
        lambda entry: tile_ref[entry],
        lambda entry: [shift_ref[entry * 3 + k] for k in range(3)],
        skew_ref,
    )
    back = beta * lax.rsqrt(norm_sq)
    rows = product + [jnp.zeros((1, member), jnp.float32)]
    spread([row * scale - back * basis_ref[own, k : k + 1, :] for k, row in enumerate(rows)], out_ref)
    second_ref[...] = second_ref[...] * scale
    lane = lax.broadcasted_iota(jnp.int32, (1, member), 1)
    scalar_ref[...] = jnp.where(lane == 0, alpha, jnp.where(lane == 1, beta, 0.0))


def last_kernel(cols, total_entries, config_ref, second_ref, image_ref, scalar_ref, mode_ref, coefficient_ref):
    own = lax.axis_index("row") * cols + lax.axis_index("col")
    member = config_ref.shape[1]
    alpha = whole_sum(second_ref, image_ref) / total_entries
    rest = image_ref[...] - alpha * second_ref[...]
    total = jnp.sum(rest * rest, axis=0)
    total = jnp.sum(jnp.sum(total, axis=0, keepdims=True), axis=1, keepdims=True)
    beta = jnp.sqrt(total / total_entries + norm_eps)
    mine = (image_ref[own] - alpha * second_ref[own]) / beta
    u = [config_ref[k : k + 1, :] for k in range(3, 6)]
    turn = cross3(u, [mine[k : k + 1] for k in range(3, 6)])
    along = mine[6:7]
    mode_ref[...] = jnp.concatenate([mine[0:3]] + [turn[k] + along * u[k] for k in range(3)], axis=0)
    lane = lax.broadcasted_iota(jnp.int32, (1, member), 1)
    coefficient_ref[...] = jnp.where(lane == 2, alpha, jnp.where(lane == 3, beta, scalar_ref[...]))


def local(config, start, tile_list, tile_count):
    dof, member = config.shape
    row_devices = lax.axis_size("row")
    col_devices = lax.axis_size("col")
    devices = row_devices * col_devices
    total_entries = float(dof * member * devices)
    period = (5.0, 5.0, 3.5 * (member // 16))
    entries = tile_list[0, 0]
    slots, fields = entries.shape
    longest = (row_devices + col_devices) * slots + 1

    def shaped(*shape):
        return jax.ShapeDtypeStruct(shape, jnp.float32)

    def everywhere(copies):
        return lax.all_to_all(copies, ("row", "col"), 0, 0, tiled=True)

    params = pltpu.CompilerParams(vmem_limit_bytes=VMEM_LIMIT)
    vmem = pl.BlockSpec(memory_space=pltpu.VMEM)
    smem = pl.BlockSpec(memory_space=pltpu.SMEM)

    in_use = jnp.arange(slots, dtype=jnp.int32) < tile_count[0, 0]
    fields_f = jnp.where(in_use[:, None], entries, -9).astype(jnp.float32).T.reshape(1, fields * slots)
    list_row = jnp.pad(fields_f, ((0, 0), (0, member - fields * slots)), constant_values=-9.0)

    packed = pl.pallas_call(
        pack_kernel,
        out_shape=shaped(devices, ROWS, member),
        in_specs=[vmem] * 3,
        out_specs=vmem,
        compiler_params=params,
    )(config, start, list_row)
    together = everywhere(packed)

    image, tiles, shifts, count = pl.pallas_call(
        functools.partial(first_kernel, row_devices, col_devices, period),
        out_shape=(
            shaped(devices, SUB, member),
            jax.ShapeDtypeStruct((longest,), jnp.int32),
            shaped(longest * 3),
            jax.ShapeDtypeStruct((1,), jnp.int32),
        ),
        in_specs=[vmem],
        out_specs=(vmem, smem, smem, smem),
        scratch_shapes=[
            pltpu.VMEM((12, SUB, member), jnp.float32),
            pltpu.VMEM((row_devices + col_devices, member), jnp.int32),
            pltpu.SMEM((row_devices + col_devices, member), jnp.int32),
            pltpu.SemaphoreType.DMA,
        ],
        compiler_params=params,
    )(together)
    image = everywhere(image)

    residual, second, scalars = pl.pallas_call(
        functools.partial(second_kernel, col_devices, total_entries),
        out_shape=(shaped(devices, SUB, member), shaped(devices, SUB, member), shaped(1, member)),
        in_specs=[smem, smem, smem, vmem, vmem],
        out_specs=(vmem, vmem, vmem),
        scratch_shapes=[pltpu.VMEM((12, SUB, member), jnp.float32), pltpu.VMEM((devices, SUB, member), jnp.float32)],
        compiler_params=params,
    )(tiles, shifts, count, together, image)
    residual = everywhere(residual)

    mode, coefficients = pl.pallas_call(
        functools.partial(last_kernel, col_devices, total_entries),
        out_shape=(shaped(dof, member), shaped(1, member)),
        in_specs=[vmem] * 4,
        out_specs=(vmem, vmem),
        compiler_params=params,
    )(config, second, residual, scalars)
    return (coefficients[0, :4], mode)


def solution(mesh):
    placed = (
        P(None, ("row", "col")),
        P(None, ("row", "col")),
        P("row", "col", None, None),
        P("row", "col"),
    )
    return jax.shard_map(
        local, mesh=mesh, in_specs=placed, out_specs=(P(), P(None, ("row", "col"))), check_vma=False
    )
```

time: 399 us -> 98.3 us (0.25)
  blocking collectives: 216 us -> 68.4 us
  other arithmetic: 100 us -> 0.08 us
  loops' own time: 65.7 us -> 0 us
  Pallas kernels: 0 us -> 27 us
  local copies, waits for them, and re-layouts: 14.9 us -> 1.37 us
    all_gather x3 -> x0, blocking collectives: 117 us -> none  [everywhere(): gathered = lax.all_gather(values, ('row', 'col'), axis=0, tiled=False)]
    unnamed x4 -> x0, blocking collectives: 98.9 us -> none
    all_to_all x0 -> x3, blocking collectives: none -> 68.4 us  [everywhere(): return lax.all_to_all(copies, ('row', 'col'), 0, 0, tiled=True)]
    another operation x2 -> x0, loops' own time: 65.7 us -> none  [apply_hessian(): lax.fori_loop(0, used, visit, (jnp.zeros_like(row_vectors), jnp.zeros_lik...]
    reduce_sum x131 -> x0, other arithmetic: 28.8 us -> none  [the longest x32 13.8 us: pair_energy(): along_right = jnp.sum(direction * right_axis, axis=0)]
    pallas_call x0 -> x4, Pallas kernels: none -> 27 us  [the longest x1 15.1 us: local(): pl.pallas_call(functools.partial(first_kernel, row_devices, col_devices,...]
    add_any x111 -> x0, other arithmetic: 24.5 us -> none  [the longest x14 9.53 us: pair_energy(): chi_shape * cosine]
    another operation x29 -> x0, other arithmetic: 21.3 us -> none
where the time goes in v4:
time: 98.3 us; the launch traced here: 98.2 us
  blocking collectives  68.4 us (70%)
  Pallas kernels  27 us (27%)
  local copies, waits for them, and re-layouts  1.37 us (1%)
  between operations  1.34 us (1%)
    all_to_all x3, blocking collectives, everywhere(): return lax.all_to_all(copies, ('row', 'col'), 0, 0, tiled=True)  68.4 us
    pallas_call x1, Pallas kernels, local(): pl.pallas_call(functools.partial(first_kernel, row_devices, col_devices,...  15.1 us
    pallas_call x1, Pallas kernels, local(): pl.pallas_call(functools.partial(second_kernel, col_devices, total_entrie...  11 us

profile of v4, /device:TPU:0, one launch (start us, length us, event | category | flops | bytes accessed | tf_op | source)
XLA Modules:
  0.0 98.2 jit_solution(1331950205239303863)
XLA Ops:
  0.6 0.0 copy-start.2
  1.3 0.0 copy-done.2
  1.3 0.1 copy.6
  1.4 0.1 fusion.1
  1.5 0.0 copy-start.1
  1.5 0.1 copy.7
  1.6 0.0 copy-start
  1.6 0.1 reshape.11
  1.7 0.5 copy-done.1
  2.2 0.1 copy-done
  2.3 17.7 %all_to_all.15.all_ref = f32[32,16,128]{2,1,0:T(8,128)S(1)} all-to-all(f32[32,16,128]{2,1,0:T(8,128)S(1)} %shard_map.59), channel_id=1, replica_groups=mesh['row'=4,'col'=8] {'row','col'}, dimensions={0} | all-to-all | bytes 524288 | tf_op jit(solution)/shard_map/all_to_all | solution.py:336
  20.0 15.1 %shard_map.60 = (f32[32,8,128]{2,1,0:T(8,128)S(1)}, s32[97]{0:T(128)S(1)}, f32[291]{0:T(512)S(1)}, s32[1]{0:T(128)}) custom-call(f32[32,16,128]{2,1,0:T(8,128)S(1)} %all_to_all.15.all_ref), custom_call_target="tpu_custom_call" | custom-call | tf_op jit(solution)/shard_map/pallas_call | solution.py:355
  35.1 25.2 %all_to_all.16.image_ref = f32[32,8,128]{2,1,0:T(8,128)S(1)} all-to-all(f32[32,8,128]{2,1,0:T(8,128)S(1)} %get-tuple-element.14), channel_id=1, replica_groups=mesh['row'=4,'col'=8] {'row','col'}, dimensions={0} | all-to-all | bytes 262144 | tf_op jit(solution)/shard_map/all_to_all | solution.py:336
  60.4 11.0 %shard_map.61 = (f32[32,8,128]{2,1,0:T(8,128)S(1)}, f32[32,8,128]{2,1,0:T(8,128)S(1)}, f32[1,128]{1,0:T(1,128)S(1)}) custom-call(s32[97]{0:T(128)S(1)} %get-tuple-element.11.tile_ref, f32[291]{0:T(512)S(1)} %get-tuple-element.12.shift_ref, s32[1]{0:T(128)} %get-tuple-element.13.count_ref, f32[32,16,128]{2,1,0:T(8,128)S(1)} %all_to_all.15.all_ref, ...), custom_call_target="tpu_custom_call" | custom-call | tf_op jit(solution)/shard_map/pallas_call | solution.py:375
  71.3 25.5 %all_to_all.17.image_ref = f32[32,8,128]{2,1,0:T(8,128)S(1)} all-to-all(f32[32,8,128]{2,1,0:T(8,128)S(1)} %get-tuple-element.16), channel_id=1, replica_groups=mesh['row'=4,'col'=8] {'row','col'}, dimensions={0} | all-to-all | bytes 262144 | tf_op jit(solution)/shard_map/all_to_all | solution.py:336
  96.8 0.9 shard_map.62
  97.7 0.5 slice_bitcast_fusion
  (3 shorter events, 0.0 us)
Async XLA Ops:
  0.6 0.7 copy-start.2
  1.5 0.7 copy-start.1
  1.6 0.7 copy-start

commit v5 on v4

--- a/solution.py
+++ b/solution.py
@@ -18,6 +18,8 @@
 FRAME = 8
 LIST_ROW = 14
 ROWS = 16
+CODE_BITS = 6
+GROUP = 2
 VMEM_LIMIT = 48 * 1024 * 1024
 
 
@@ -135,8 +137,57 @@
     return a, c, u_r, u_a, u_b, u_c, du_r, du_a, du_b, du_c
 
 
-def tile_product(count, own, frame, moved, entry_tile, entry_shift, skew_ref):
-    member = frame(own, 0).shape[1]
+def offsets_of(code, period):
+    return [((code >> bits & 3) - 1).astype(jnp.float32) * size for bits, size in zip((4, 2, 0), period)]
+
+
+def skew_entry(entry, code, period, frame, moved, skew_ref):
+    partner = code >> CODE_BITS
+    shift = offsets_of(code, period)
+    member = skew_ref.shape[3]
+    sublane = lax.broadcasted_iota(jnp.int32, (SUB, member), 0)
+
+    def skewed(row):
+        block = jnp.broadcast_to(row, (SUB, member))
+        for bit in (1, 2, 4):
+            block = jnp.where((sublane & bit) > 0, pltpu.roll(block, bit, 1), block)
+        return block
+
+    for k in range(3):
+        skew_ref[entry, k] = skewed(frame(partner, k)) + shift[k]
+        skew_ref[entry, 3 + k] = skewed(frame(partner, 3 + k))
+        skew_ref[entry, 6 + k] = skewed(moved(partner, k))
+        skew_ref[entry, 9 + k] = skewed(moved(partner, 3 + k))
+
+
+def near_blocks(code, period, own_frame, partner_frame):
+    member = own_frame.shape[1]
+    row = lax.broadcasted_iota(jnp.int32, (SUB, member), 0)
+    shift = offsets_of(code, period)
+    sign = jnp.where(row < 3, 1.0, jnp.where(row < 6, -1.0, 0.0))
+
+    def doubled(block):
+        centre = jnp.where(row < 3, block, 0.0)
+        return centre + pltpu.roll(centre, 3, 0)
+
+    moved = jnp.where(row % 3 == 0, shift[0], jnp.where(row % 3 == 1, shift[1], shift[2]))
+    box = (doubled(partner_frame) + moved) * sign
+    for bit in (1, 2, 4):
+        box = jnp.maximum(box, pltpu.roll(box, bit, 1))
+    here = doubled(own_frame) * sign
+    blocks = member // SUB
+    reach = []
+    for k in range(blocks):
+        gap = jnp.maximum(here - (pltpu.roll(box, k * SUB, 1) if k else box), 0.0)
+        reach.append(jnp.sum(gap * gap, axis=0, keepdims=True))
+    nearest = jnp.min(jnp.concatenate(reach, axis=0), axis=1, keepdims=True)
+    weight = (1 << lax.broadcasted_iota(jnp.int32, (blocks, 1), 0)).astype(jnp.float32)
+    return jnp.sum(jnp.where(nearest < cutoff_sq * 1.001, weight, 0.0)).astype(jnp.int32)
+
+
+def tile_product(item_count, item_ref, own, frame, moved, skew_ref):
+    member = skew_ref.shape[3]
+    blocks = member // SUB
 
     def wide(row):
         return jnp.broadcast_to(row, (SUB, member))
@@ -147,41 +198,29 @@
     dui = [wide(moved(own, k)) for k in range(3, 6)]
     first_row = (lax.broadcasted_iota(jnp.int32, (SUB, member), 0) == 0).astype(jnp.float32)
 
-    sublane = lax.broadcasted_iota(jnp.int32, (SUB, member), 0)
-
-    def skewed(row):
-        block = wide(row)
-        for bit in (1, 2, 4):
-            block = jnp.where((sublane & bit) > 0, pltpu.roll(block, bit, 1), block)
-        return block
-
-    def visit_entry(entry, totals):
-        partner = entry_tile(entry)
-        shift = entry_shift(entry)
-        for k in range(3):
-            skew_ref[k] = skewed(frame(partner, k)) + shift[k]
-        for k in range(3, 6):
-            skew_ref[k] = skewed(frame(partner, k))
-        for k in range(6):
-            skew_ref[6 + k] = skewed(moved(partner, k))
-        return lax.fori_loop(0, member // SUB, functools.partial(visit, entry), totals)
-
-    def visit(entry, block, totals):
-        other = [pltpu.roll(skew_ref[k], block * SUB, 1) for k in range(12)]
+    def one(at):
+        item = item_ref[at]
+        entry = item // blocks
+        turn_by = item % blocks * SUB
+        other = [pltpu.roll(skew_ref[entry, k], turn_by, 1) for k in range(12)]
         d = [other[k] - xi[k] for k in range(3)]
         uj = other[3:6]
         dd = [other[6 + k] - dxi[k] for k in range(3)]
         duj = other[9:12]
-        item = entry * (member // SUB) + block
-        lift = first_row * jnp.where(item == 0, 2.0 * cutoff_sq, 0.0)
+        itself = jnp.where(item == 0, 2.0 * cutoff_sq, 0.0)
+        unused = jnp.where(at < item_count, 0.0, 2.0 * cutoff_sq)
+        lift = first_row * itself + unused
         a, c, u_r, u_a, u_b, u_c, du_r, du_a, du_b, du_c = pair_tangent(d, ui, uj, dd, dui, duj, lift)
         force = [du_r * d[k] + u_r * dd[k] + du_b * uj[k] + u_b * duj[k] for k in range(3)]
         turn = [du_a * d[k] + u_a * dd[k] + du_c * uj[k] + u_c * duj[k] for k in range(3)]
-        news = force + turn + [du_a, u_a, u_a * a + u_c * c]
-        return tuple(total + new for total, new in zip(totals, news))
+        return force + turn + [du_a, u_a, u_a * a + u_c * c]
+
+    def visit(step, totals):
+        news = [one(step * GROUP + part) for part in range(GROUP)]
+        return tuple(sum(parts, total) for total, parts in zip(totals, zip(*news)))
 
     zero = jnp.zeros((SUB, member), jnp.float32)
-    totals = lax.fori_loop(0, count, visit_entry, (zero,) * 9)
+    totals = lax.fori_loop(0, (item_count + GROUP - 1) // GROUP, visit, (zero,) * 9)
     sums = [jnp.sum(total, axis=0, keepdims=True) for total in totals]
     u = [row[:1] for row in ui]
     t = [row[:1] for row in dui]
@@ -208,19 +247,21 @@
     out_ref[...] = jnp.broadcast_to(block[None], out_ref.shape)
 
 
-def first_kernel(rows, cols, period, all_ref, out_ref, tile_ref, shift_ref, count_ref, skew_ref, code_ref, code_smem, sem):
+def first_kernel(
+    rows, cols, slots, period, all_ref, out_ref, entry_ref, item_ref, count_ref, skew_ref, code_ref, code_smem, sem
+):
     member = all_ref.shape[2]
     row_id = lax.axis_index("row")
     col_id = lax.axis_index("col")
     own = row_id * cols + col_id
-    slots = SUB
+    blocks = member // SUB
 
     def field(line, at):
         return line if at == 0 else pltpu.roll(line, member - at * slots, 1)
 
     def encode(line, partner, side):
-        offset = (field(line, 2) * 9.0 + field(line, 3) * 3.0 + field(line, 4)) * side + 13.0
-        return partner * 27.0 + offset
+        offset = (field(line, 2) * 16.0 + field(line, 3) * 4.0 + field(line, 4)) * side + 21.0
+        return partner * float(1 << CODE_BITS) + offset
 
     row_f = row_id.astype(jnp.float32)
     col_f = col_id.astype(jnp.float32)
@@ -237,35 +278,39 @@
     copy.start()
     copy.wait()
 
-    tile_ref[0] = own
-    for k in range(3):
-        shift_ref[k] = 0.0
-
-    def gather(at, count):
-        code = code_smem[at // slots, at % slots]
-
-        @pl.when(code >= 0)
-        def _():
-            offset = code % 27
-            tile_ref[count] = code // 27
-            shift_ref[count * 3] = (offset // 9 - 1).astype(jnp.float32) * period[0]
-            shift_ref[count * 3 + 1] = (offset // 3 % 3 - 1).astype(jnp.float32) * period[1]
-            shift_ref[count * 3 + 2] = (offset % 3 - 1).astype(jnp.float32) * period[2]
-
-        return count + (code >= 0).astype(jnp.int32)
-
-    count = lax.fori_loop(0, (rows + cols) * slots, gather, jnp.int32(1))
-    count_ref[0] = count
-    product = tile_product(
-        count,
-        own,
-        lambda tile, k: all_ref[tile, FRAME + k : FRAME + k + 1, :],
-        lambda tile, k: all_ref[tile, k : k + 1, :],
-        lambda entry: tile_ref[entry],
-        lambda entry: [shift_ref[entry * 3 + k] for k in range(3)],
-        skew_ref,
-    )
-    spread(product, out_ref)
+    entry_ref[0] = own * (1 << CODE_BITS) + 21
+
+    def gather(line, count):
+        for slot in range(slots):
+            code = code_smem[line, slot]
+            entry_ref[count] = code
+            count = count + (code >= 0).astype(jnp.int32)
+        return count
+
+    entries = lax.fori_loop(0, rows + cols, gather, jnp.int32(1))
+    own_frame = all_ref[own, FRAME : FRAME + SUB, :]
+
+    def frame(tile, k):
+        return all_ref[tile, FRAME + k : FRAME + k + 1, :]
+
+    def moved(tile, k):
+        return all_ref[tile, k : k + 1, :]
+
+    def prepare(entry, count):
+        code = entry_ref[entry]
+        skew_entry(entry, code, period, frame, moved, skew_ref)
+        bits = near_blocks(code, period, own_frame, all_ref[code >> CODE_BITS, FRAME : FRAME + SUB, :])
+        for block in range(blocks):
+            item_ref[count] = entry * blocks + block
+            count = count + (bits >> block & 1)
+        return count
+
+    items = lax.fori_loop(0, entries, prepare, jnp.int32(0))
+    for part in range(GROUP):
+        item_ref[items + part] = 0
+    count_ref[0] = entries
+    count_ref[1] = items
+    spread(tile_product(items, item_ref, own, frame, moved, skew_ref), out_ref)
 
 
 def whole_sum(left_ref, right_ref):
@@ -274,7 +319,19 @@
 
 
 def second_kernel(
-    cols, total_entries, tile_ref, shift_ref, count_ref, all_ref, image_ref, out_ref, second_ref, scalar_ref, skew_ref, basis_ref
+    cols,
+    total_entries,
+    period,
+    entry_ref,
+    item_ref,
+    count_ref,
+    all_ref,
+    image_ref,
+    out_ref,
+    second_ref,
+    scalar_ref,
+    skew_ref,
+    basis_ref,
 ):
     own = lax.axis_index("row") * cols + lax.axis_index("col")
     member = all_ref.shape[2]
@@ -284,15 +341,19 @@
     second_ref[...] = image_ref[...] - alpha * basis_ref[...]
     beta = jnp.sqrt(whole_sum(second_ref, second_ref) / total_entries / norm_sq + norm_eps)
     scale = lax.rsqrt(norm_sq) / beta
-    product = tile_product(
-        count_ref[0],
-        own,
-        lambda tile, k: all_ref[tile, FRAME + k : FRAME + k + 1, :],
-        lambda tile, k: second_ref[tile, k : k + 1, :],
-        lambda entry: tile_ref[entry],
-        lambda entry: [shift_ref[entry * 3 + k] for k in range(3)],
-        skew_ref,
-    )
+
+    def frame(tile, k):
+        return all_ref[tile, FRAME + k : FRAME + k + 1, :]
+
+    def moved(tile, k):
+        return second_ref[tile, k : k + 1, :]
+
+    def prepare(entry, carry):
+        skew_entry(entry, entry_ref[entry], period, frame, moved, skew_ref)
+        return carry
+
+    lax.fori_loop(0, count_ref[0], prepare, 0)
+    product = tile_product(count_ref[1], item_ref, own, frame, moved, skew_ref)
     back = beta * lax.rsqrt(norm_sq)
     rows = product + [jnp.zeros((1, member), jnp.float32)]
     spread([row * scale - back * basis_ref[own, k : k + 1, :] for k, row in enumerate(rows)], out_ref)
@@ -352,18 +413,19 @@
     )(config, start, list_row)
     together = everywhere(packed)
 
-    image, tiles, shifts, count = pl.pallas_call(
-        functools.partial(first_kernel, row_devices, col_devices, period),
+    skew = pltpu.VMEM((longest, 12, SUB, member), jnp.float32)
+    image, codes, items, counts = pl.pallas_call(
+        functools.partial(first_kernel, row_devices, col_devices, slots, period),
         out_shape=(
             shaped(devices, SUB, member),
-            jax.ShapeDtypeStruct((longest,), jnp.int32),
-            shaped(longest * 3),
-            jax.ShapeDtypeStruct((1,), jnp.int32),
+            jax.ShapeDtypeStruct((longest + 1,), jnp.int32),
+            jax.ShapeDtypeStruct((longest * (member // SUB) + GROUP,), jnp.int32),
+            jax.ShapeDtypeStruct((2,), jnp.int32),
         ),
         in_specs=[vmem],
         out_specs=(vmem, smem, smem, smem),
         scratch_shapes=[
-            pltpu.VMEM((12, SUB, member), jnp.float32),
+            skew,
             pltpu.VMEM((row_devices + col_devices, member), jnp.int32),
             pltpu.SMEM((row_devices + col_devices, member), jnp.int32),
             pltpu.SemaphoreType.DMA,
@@ -373,13 +435,13 @@
     image = everywhere(image)
 
     residual, second, scalars = pl.pallas_call(
-        functools.partial(second_kernel, col_devices, total_entries),
+        functools.partial(second_kernel, col_devices, total_entries, period),
         out_shape=(shaped(devices, SUB, member), shaped(devices, SUB, member), shaped(1, member)),
         in_specs=[smem, smem, smem, vmem, vmem],
         out_specs=(vmem, vmem, vmem),
-        scratch_shapes=[pltpu.VMEM((12, SUB, member), jnp.float32), pltpu.VMEM((devices, SUB, member), jnp.float32)],
+        scratch_shapes=[skew, pltpu.VMEM((devices, SUB, member), jnp.float32)],
         compiler_params=params,
-    )(tiles, shifts, count, together, image)
+    )(codes, items, counts, together, image)
     residual = everywhere(residual)
 
     mode, coefficients = pl.pallas_call(

time: 98.3 us -> 67.9 us (0.69)
  blocking collectives: 68.4 us -> 52.1 us
  Pallas kernels: 27 us -> 12.9 us
    all_to_all x3, blocking collectives: 68.4 us -> 52.1 us  [everywhere(): return lax.all_to_all(copies, ('row', 'col'), 0, 0, tiled=True)]
    pallas_call x1, Pallas kernels: 15.1 us -> 7.19 us  [local(): pl.pallas_call(functools.partial(first_kernel, row_devices, col_devices,...]
    pallas_call x1, Pallas kernels: 11 us -> 4.81 us  [local(): pl.pallas_call(functools.partial(second_kernel, col_devices, total_entrie...]
where the time goes in v5:
time: 67.9 us; the launch traced here: 67.7 us
  blocking collectives  52.1 us (77%)
  Pallas kernels  12.9 us (19%)
  local copies, waits for them, and re-layouts  1.37 us (2%)
  between operations  1.34 us (2%)
    all_to_all x3, blocking collectives, everywhere(): return lax.all_to_all(copies, ('row', 'col'), 0, 0, tiled=True)  52.1 us
    pallas_call x1, Pallas kernels, local(): pl.pallas_call(functools.partial(first_kernel, row_devices, col_devices,...  7.19 us
    pallas_call x1, Pallas kernels, local(): pl.pallas_call(functools.partial(second_kernel, col_devices, total_entrie...  4.81 us

profile of v5, /device:TPU:0, one launch (start us, length us, event | category | flops | bytes accessed | tf_op | source)
XLA Modules:
  0.0 67.7 jit_solution(11781533301547375677)
XLA Ops:
  0.6 0.0 copy-start.2
  1.3 0.0 copy-done.2
  1.3 0.1 copy.6
  1.4 0.1 fusion.1
  1.5 0.0 copy-start.1
  1.5 0.1 copy.7
  1.6 0.0 copy-start
  1.6 0.1 reshape.11
  1.7 0.5 copy-done.1
  2.2 0.1 copy-done
  2.3 17.7 %all_to_all.15.all_ref = f32[32,16,128]{2,1,0:T(8,128)S(1)} all-to-all(f32[32,16,128]{2,1,0:T(8,128)S(1)} %shard_map.59), channel_id=1, replica_groups=mesh['row'=4,'col'=8] {'row','col'}, dimensions={0} | all-to-all | bytes 524288 | tf_op jit(solution)/shard_map/all_to_all | solution.py:397
  20.0 7.2 %shard_map.60 = (f32[32,8,128]{2,1,0:T(8,128)S(1)}, s32[98]{0:T(128)S(1)}, s32[1554]{0:T(1024)S(1)}, s32[2]{0:T(128)S(1)}) custom-call(f32[32,16,128]{2,1,0:T(8,128)S(1)} %all_to_all.15.all_ref), custom_call_target="tpu_custom_call" | custom-call | tf_op jit(solution)/shard_map/pallas_call | solution.py:417
  27.2 18.1 %all_to_all.16.image_ref = f32[32,8,128]{2,1,0:T(8,128)S(1)} all-to-all(f32[32,8,128]{2,1,0:T(8,128)S(1)} %get-tuple-element.14), channel_id=1, replica_groups=mesh['row'=4,'col'=8] {'row','col'}, dimensions={0} | all-to-all | bytes 262144 | tf_op jit(solution)/shard_map/all_to_all | solution.py:397
  45.3 4.8 %shard_map.61 = (f32[32,8,128]{2,1,0:T(8,128)S(1)}, f32[32,8,128]{2,1,0:T(8,128)S(1)}, f32[1,128]{1,0:T(1,128)S(1)}) custom-call(s32[98]{0:T(128)S(1)} %get-tuple-element.11.entry_ref, s32[1554]{0:T(1024)S(1)} %get-tuple-element.12.item_ref, s32[2]{0:T(128)S(1)} %get-tuple-element.13.count_ref, f32[32,16,128]{2,1,0:T(8,128)S(1)} %all_to_all.15.all_ref, ...), custom_call_target="tpu_custom_call" | custom-call | tf_op jit(solution)/shard_map/pallas_call | solution.py:437
  50.1 16.3 %all_to_all.17.image_ref = f32[32,8,128]{2,1,0:T(8,128)S(1)} all-to-all(f32[32,8,128]{2,1,0:T(8,128)S(1)} %get-tuple-element.16), channel_id=1, replica_groups=mesh['row'=4,'col'=8] {'row','col'}, dimensions={0} | all-to-all | bytes 262144 | tf_op jit(solution)/shard_map/all_to_all | solution.py:397
  66.4 0.9 %shard_map.62 = (f32[6,128]{1,0:T(8,128)}, f32[1,128]{1,0:T(1,128)S(1)}) custom-call(f32[6,128]{1,0:T(8,128)S(1)} %copy-done, f32[32,8,128]{2,1,0:T(8,128)S(1)} %get-tuple-element.15.second_ref, f32[32,8,128]{2,1,0:T(8,128)S(1)} %all_to_all.17.image_ref, f32[1,128]{1,0:T(1,128)S(1)} %get-tuple-element.17.scalar_ref), custom_call_target="tpu_custom_call" | custom-call | tf_op jit(solution)/shard_map/pallas_call | solution.py:447
  67.2 0.5 slice_bitcast_fusion
  (3 shorter events, 0.0 us)
Async XLA Ops:
  0.6 0.7 %copy-start.2 = (s32[1,1,8,5]{2,1,3,0:T(1,128)S(1)}, s32[1,1,8,5]{2,1,3,0:T(1,128)}, u32[]{:S(2)}) copy-start(s32[1,1,8,5]{2,1,3,0:T(1,128)} %param.6) | copy-start | bytes 484
  1.5 0.7 %copy-start.1 = (f32[6,128]{1,0:T(8,128)S(1)}, f32[6,128]{1,0:T(8,128)}, u32[]{:S(2)}) copy-start(f32[6,128]{1,0:T(8,128)} %start_ref.1) | copy-start | bytes 9220
  1.6 0.7 %copy-start = (f32[6,128]{1,0:T(8,128)S(1)}, f32[6,128]{1,0:T(8,128)}, u32[]{:S(2)}) copy-start(f32[6,128]{1,0:T(8,128)} %config_ref.3) | copy-start | bytes 9220
